TPU v7x, 32 devices: a whole 2x2x4 slice. The times are simulated.
32 devices in a mesh: lat: 4 (over y, core), lon: 8 (over z, x).
Axes of the slice: x: 2, y: 2, z: 4, core: 2. Of those that a mesh axis runs over, the one named last changes fastest.
Arguments:
- control: float32 [512, 1024, 128], P('lat', 'lon'), may hold values from -6 to 6
- corr_blocks: float32 [9, 128, 128], replicated, may hold values from -0.1875 to 0.1875
- jacobian: float32 [128, 128], replicated, may hold values from -0.5 to 0.5
- obs_values: bfloat16 [65536, 128], P(('lat', 'lon')), may hold values from -6 to 6
- obs_count: int32 [32, 32], P(('lat', 'lon')), may hold values from 16 to 64, as said below
- obs_col: int32 [32, 2048], P(('lat', 'lon')), may hold values from 0 to 16254, as said below
- obs_frac: float32 [32, 2, 2048], P(('lat', 'lon')), may hold values from 0 to 1
- obs_rinv: float32 [32, 2048], P(('lat', 'lon')), may hold values from 0.25 to 4
Outputs:
- gradient: float32 [512, 1024, 128], P('lat', 'lon')
- weighted_dep: bfloat16 [65536, 128], P(('lat', 'lon'))
Inputs may be any that keep to these rules, and one draw needn't show every extreme that they name: `obs_count`: every source fills all 64 slots for at least one owner, and one owner receives 64 from every source. `obs_col`: i * 128 + j with i < 127 and j < 127, so the 2 x 2 stencil lies in the owner's block; entries of dead slots are valid too.
All inputs are finite; a program needn't handle non-finite values.
Results may differ from a plain program's by a relative error of at most 0.001.
Values may be sent and summed in bfloat16 or wider, within the bound.
A program may use at most 192 MiB of HBM per device.

v0:
```python
import jax
import jax.numpy as jnp
from jax import lax
from jax.sharding import PartitionSpec as P

CLAT = 128
CLON = 128
LEV = 128
CH = 128
CAP = 64


def with_halo(array, sides, width):
    for axis, dim in sides:
        peers, length = (lax.axis_size(axis), array.shape[dim])
        up = [(i, (i + 1) % peers) for i in range(peers - 1)]
        down = [(j, i) for i, j in up]
        last = lax.slice_in_dim(array, length - width, length, axis=dim)
        initial = lax.slice_in_dim(array, 0, width, axis=dim)
        before = lax.ppermute(last, axis, up)
        after = lax.ppermute(initial, axis, down)
        array = jnp.concatenate([before, array, after], axis=dim)
    return array


def root_summed(padded, corr_blocks):
    height = padded.shape[0] - 2
    breadth = padded.shape[1] - 2
    summed = jnp.zeros((height, breadth, corr_blocks.shape[2]), jnp.float32)
    for step_lat in (-1, 0, 1):
        for step_lon in (-1, 0, 1):
            which = (step_lat + 1) * 3 + (step_lon + 1)
            piece = padded[
                1 + step_lat : 1 + step_lat + height, 1 + step_lon : 1 + step_lon + breadth
            ]
            summed = summed + jnp.einsum(
                "ijl,lm->ijm", piece, corr_blocks[which], precision=lax.Precision.HIGHEST
            )
    return summed


def transpose_summed(padded, corr_blocks):
    height = padded.shape[0] - 2
    breadth = padded.shape[1] - 2
    summed = jnp.zeros((height, breadth, corr_blocks.shape[1]), jnp.float32)
    for step_lat in (-1, 0, 1):
        for step_lon in (-1, 0, 1):
            which = (step_lat + 1) * 3 + (step_lon + 1)
            piece = padded[
                1 - step_lat : 1 - step_lat + height, 1 - step_lon : 1 - step_lon + breadth
            ]
            summed = summed + jnp.einsum(
                "ijm,lm->ijl", piece, corr_blocks[which], precision=lax.Precision.HIGHEST
            )
    return summed


def observe(state_rows, observed, counts, corners, fractions, rinv, jacobian):
    slot_count = corners.shape[0]
    frac_lat = fractions[0][:, None]
    frac_lon = fractions[1][:, None]
    weight_sw = (1.0 - frac_lat) * (1.0 - frac_lon)
    weight_se = (1.0 - frac_lat) * frac_lon
    weight_nw = frac_lat * (1.0 - frac_lon)
    weight_ne = frac_lat * frac_lon
    targets = jnp.concatenate([corners, corners + 1, corners + CLON, corners + CLON + 1])
    picked = jnp.take(state_rows, targets, axis=0)
    profile = (
        weight_sw * picked[0:slot_count]
        + weight_se * picked[slot_count : 2 * slot_count]
        + weight_nw * picked[2 * slot_count : 3 * slot_count]
        + weight_ne * picked[3 * slot_count : 4 * slot_count]
    )
    evolved = jnp.dot(profile, jacobian, precision=lax.Precision.HIGHEST)
    departure = evolved - observed.astype(jnp.float32)
    live_slot = (jnp.arange(CAP, dtype=jnp.int32)[None, :] < counts[:, None]).reshape(-1)
    weighted = jnp.where(live_slot[:, None], rinv[:, None] * departure, jnp.zeros_like(departure))
    adjoint_rows = jnp.dot(weighted, jacobian.T, precision=lax.Precision.HIGHEST)
    spread_terms = jnp.concatenate(
        [
            weight_sw * adjoint_rows,
            weight_se * adjoint_rows,
            weight_nw * adjoint_rows,
            weight_ne * adjoint_rows,
        ],
        axis=0,
    )
    increment = jax.ops.segment_sum(spread_terms, targets, num_segments=state_rows.shape[0])
    return (weighted, increment)


def body(control, corr_blocks, jacobian, obs_values, obs_count, obs_col, obs_frac, obs_rinv):
    lat_devices = lax.axis_size("lat")
    lon_devices = lax.axis_size("lon")
    n_devices = lat_devices * lon_devices
    padded = with_halo(control, (("lat", 0), ("lon", 1)), 1)
    state = root_summed(padded, corr_blocks)
    outgoing = obs_values.reshape(n_devices, CAP, CH)
    incoming = lax.all_to_all(outgoing, ("lat", "lon"), split_axis=0, concat_axis=0, tiled=True)
    weighted, increment = observe(
        state.reshape(CLAT * CLON, LEV),
        incoming.reshape(n_devices * CAP, CH),
        obs_count[0],
        obs_col[0],
        obs_frac[0],
        obs_rinv[0],
        jacobian,
    )
    rounded = weighted.astype(jnp.bfloat16)
    returned = lax.all_to_all(
        rounded.reshape(n_devices, CAP, CH), ("lat", "lon"), split_axis=0, concat_axis=0, tiled=True
    )
    padded_increment = with_halo(increment.reshape(CLAT, CLON, LEV), (("lat", 0), ("lon", 1)), 1)
    gradient = control + transpose_summed(padded_increment, corr_blocks)
    return (gradient, returned.reshape(n_devices * CAP, CH))


def solution(mesh):
    in_specs = (
        P("lat", "lon", None),
        P(),
        P(),
        P(("lat", "lon"), None),
        P(("lat", "lon"), None),
        P(("lat", "lon"), None),
        P(("lat", "lon"), None, None),
        P(("lat", "lon"), None),
    )
    out_specs = (P("lat", "lon", None), P(("lat", "lon"), None))
    return jax.shard_map(body, mesh=mesh, in_specs=in_specs, out_specs=out_specs, check_vma=False)
```

profile of v0, /device:TPU:0, one launch (start us, length us, event | category | flops | bytes accessed | tf_op | source)
XLA Modules:
  0.0 358.5 jit_solution(6239461596426532367)
XLA Ops:
  5.2 9.2 %all-to-all-start = ((bf16[32,64,128]{2,1,0:T(8,128)(2,1)}), bf16[32,64,128]{2,1,0:T(8,128)(2,1)S(1)}, u32[]{:S(2)}, u32[]{:S(2)}) async-start(bf16[32,64,128]{2,1,0:T(8,128)(2,1)} %bitcast.95), calls=%async_computation | async-start | bytes 1048576 | tf_op jit(solution)/shard_map/all_to_all | solution.py:99
  14.5 10.8 %fusion.81 = f32[128,128,128]{2,1,0:T(8,128)} fusion(f32[128,128,128]{2,1,0:T(8,128)} %param.8, f32[9,128,128]{2,1,0:T(8,128)} %param.9), kind=kOutput, calls=%fused_computation.101 | convolution fusion | flops 3221225472 | bytes 16842752 | tf_op jit(solution)/shard_map/ijl,lm->ijm/dot_general | solution.py:36
  36.2 10.8 %fusion = f32[128,128,128]{2,1,0:T(8,128)} fusion(f32[128,128,128]{2,1,0:T(8,128)} %param.8, f32[1,128,128]{2,1,0:T(8,128)S(1)} %collective-permute-done, f32[9,128,128]{2,1,0:T(8,128)S(1)} %copy-done.4), kind=kOutput, calls=%fused_computation.12 | convolution fusion | flops 3223339008 | bytes 16908288 | tf_op jit(solution)/shard_map/ijl,lm->ijm/dot_general | solution.py:36
  47.1 8.9 %fusion.4 = f32[128,128,128]{2,1,0:T(8,128)} fusion(f32[1,128,128]{2,1,0:T(8,128)S(1)} %collective-permute-done.1, f32[128,128,128]{2,1,0:T(8,128)S(1)} %bitcast.92, f32[9,128,128]{2,1,0:T(8,128)S(1)} %copy-done.4), kind=kOutput, calls=%fused_computation.16 | convolution fusion | flops 3223339008 | bytes 16908288 | tf_op jit(solution)/shard_map/ijl,lm->ijm/dot_general | solution.py:36
  55.9 8.8 %fusion.23 = f32[128,128,128]{2,1,0:T(8,128)} fusion(f32[130,128,128]{2,1,0:T(8,128)S(1)} %constant_dynamic-update-slice_fusion, f32[130,1,128]{2,1,0:T(1,128)S(1)} %collective-permute-done.2, f32[9,128,128]{2,1,0:T(8,128)S(1)} %copy-done.4), kind=kOutput, calls=%fused_computation.33 | convolution fusion | flops 3223322624 | bytes 17040384 | tf_op jit(solution)/shard_map/ijl,lm->ijm/dot_general | solution.py:36
  64.7 9.1 %fusion.26 = f32[128,128,128]{2,1,0:T(8,128)} fusion(f32[130,128,128]{2,1,0:T(8,128)S(1)} %constant_dynamic-update-slice_fusion, f32[130,1,128]{2,1,0:T(1,128)S(1)} %collective-permute-done.2, f32[9,128,128]{2,1,0:T(8,128)S(1)} %copy-done.4), kind=kOutput, calls=%fused_computation.35 | convolution fusion | flops 3223322624 | bytes 17040384 | tf_op jit(solution)/shard_map/ijl,lm->ijm/dot_general | solution.py:36
  73.8 10.2 %fusion.20 = f32[128,128,128]{2,1,0:T(8,128)} fusion(f32[130,128,128]{2,1,0:T(8,128)S(1)} %constant_dynamic-update-slice_fusion, f32[130,1,128]{2,1,0:T(1,128)S(1)} %collective-permute-done.3, f32[9,128,128]{2,1,0:T(8,128)S(1)} %copy-done.4), kind=kOutput, calls=%fused_computation.31 | convolution fusion | flops 3223322624 | bytes 17040384 | tf_op jit(solution)/shard_map/ijl,lm->ijm/dot_general | solution.py:36
  84.0 10.7 %fusion.17 = f32[128,128,128]{2,1,0:T(8,128)} fusion(f32[130,128,128]{2,1,0:T(8,128)S(1)} %constant_dynamic-update-slice_fusion, f32[130,1,128]{2,1,0:T(1,128)S(1)} %collective-permute-done.3, f32[9,128,128]{2,1,0:T(8,128)S(1)} %copy-done.4), kind=kOutput, calls=%fused_computation.29 | convolution fusion | flops 3223322624 | bytes 17040384 | tf_op jit(solution)/shard_map/ijl,lm->ijm/dot_general | solution.py:36
  94.8 8.8 %fusion.42 = f32[128,128,128]{2,1,0:T(8,128)} fusion(f32[130,128,128]{2,1,0:T(8,128)S(1)} %constant_dynamic-update-slice_fusion, f32[130,1,128]{2,1,0:T(1,128)S(1)} %collective-permute-done.2, f32[9,128,128]{2,1,0:T(8,128)S(1)} %copy-done.4), kind=kOutput, calls=%fused_computation.52 | convolution fusion | flops 3223322624 | bytes 17040384 | tf_op jit(solution)/shard_map/ijl,lm->ijm/dot_general | solution.py:36
  103.6 28.6 %add_add_fusion.1 = f32[128,128,128]{2,1,0:T(8,128)} fusion(f32[128,128,128]{2,1,0:T(8,128)} %fusion.4, f32[128,128,128]{2,1,0:T(8,128)} %fusion.42, f32[128,128,128]{2,1,0:T(8,128)} %fusion.17, f32[128,128,128]{2,1,0:T(8,128)} %fusion.81, f32[128,128,128]{2,1,0:T(8,128)} %fusion.23, f32[128,128,128]{2,1,0:T(8,128)} %fusion.20, ...), kind=kOutput, calls=%fused_computation.55 | convolution fusion | flops 3240099840 | bytes 84149248 | tf_op jit(solution)/shard_map/ijl,lm->ijm/dot_general | solution.py:36
  132.2 31.1 %gather_fusion = f32[8192,128]{1,0:T(8,128)} fusion(f32[16384,128]{1,0:T(8,128)} %bitcast.93, s32[8192]{0:T(1024)S(1)} %broadcast_clamp_fusion), kind=kCustom, calls=%fused_computation | custom fusion | bytes 8421376 | tf_op jit(solution)/shard_map/jit(_take)/gather | solution.py:67
  163.3 7.5 %broadcast_select_fusion = f32[8192,128]{1,0:T(8,128)} fusion(f32[8192,128]{1,0:T(8,128)} %gather_fusion, pred[8192]{0:T(1024)(128)(4,1)S(1)} %compare_and_fusion), kind=kLoop, calls=%fused_computation.68 | loop fusion | flops 1048576 | bytes 8396800 | tf_op jit(solution)/shard_map/jit(_take)/select_n | solution.py:67
  170.7 5.5 %fusion.122 = (bf16[2048,128]{1,0:T(8,128)(2,1)}, f32[2048,128]{1,0:T(8,128)S(1)}) fusion(bf16[2048,128]{1,0:T(8,128)(2,1)S(1)} %bitcast.96, f32[128,128]{1,0:T(8,128)S(1)} %copy-done, f32[8192,128]{1,0:T(8,128)} %broadcast_select_fusion, f32[2048]{0:T(1024)S(1)} %get-tuple-element.18, f32[2048]{0:T(1024)S(1)} %get-tuple-element.17, ...), kind=kOutput, calls=%fused_computation.155 | convolution fusion | flops 405798912 | bytes 6400000 | tf_op jit(solution)/shard_map/dot_general | solution.py:74
  178.9 48.4 %scatter_custom_fusion = f32[16384,128]{1,0:T(8,128)} fusion(s32[8192]{0:T(1024)S(1)} %pad_add_fusion, f32[2048,128]{1,0:T(8,128)S(1)} %get-tuple-element.13, f32[]{:T(128)} %constant.31, f32[2048,128]{1,0:T(8,128)S(1)} %get-tuple-element.14, f32[2048,128]{1,0:T(8,128)} %get-tuple-element.15, f32[2048,128]{1,0:T(8,128)S(1)} %get-tuple-element.12, ...), kind=kCustom, calls=%fused_computation.56 | custom fusion | flops 4194304 | bytes 12582920 | tf_op jit(solution)/shard_map/scatter-add | solution.py:88
  232.6 10.8 %fusion.79 = f32[128,128,128]{2,1,0:T(8,128)} fusion(f32[128,128,128]{2,1,0:T(8,128)} %bitcast.84, f32[9,128,128]{2,1,0:T(8,128)} %param.9), kind=kOutput, calls=%fused_computation.99 | convolution fusion | flops 3221225472 | bytes 16842752 | tf_op jit(solution)/shard_map/ijm,lm->ijl/dot_general | solution.py:52
  243.4 5.8 %all-to-all-start.1 = ((bf16[32,64,128]{2,1,0:T(8,128)(2,1)}), bf16[32,64,128]{2,1,0:T(8,128)(2,1)S(1)}, u32[]{:S(2)}, u32[]{:S(2)}) async-start(bf16[32,64,128]{2,1,0:T(8,128)(2,1)} %bitcast.34), calls=%async_computation.1 | async-start | bytes 1048576 | tf_op jit(solution)/shard_map/all_to_all | solution.py:110
  256.7 11.0 %fusion.8 = f32[128,128,128]{2,1,0:T(8,128)} fusion(f32[1,128,128]{2,1,0:T(8,128)S(1)} %collective-permute-done.5, f32[128,128,128]{2,1,0:T(8,128)} %bitcast.86, f32[9,128,128]{2,1,0:T(8,128)S(1)} %copy-done.5), kind=kOutput, calls=%fused_computation.20 | convolution fusion | flops 3223339008 | bytes 16908288 | tf_op jit(solution)/shard_map/ijm,lm->ijl/dot_general | solution.py:52
  267.7 8.9 %fusion.12 = f32[128,128,128]{2,1,0:T(8,128)} fusion(f32[128,128,128]{2,1,0:T(8,128)S(1)} %bitcast.89, f32[1,128,128]{2,1,0:T(8,128)S(1)} %collective-permute-done.4, f32[9,128,128]{2,1,0:T(8,128)S(1)} %copy-done.5), kind=kOutput, calls=%fused_computation.24 | convolution fusion | flops 3223339008 | bytes 16908288 | tf_op jit(solution)/shard_map/ijm,lm->ijl/dot_general | solution.py:52
  280.5 9.0 %fusion.30 = f32[128,128,128]{2,1,0:T(8,128)} fusion(f32[130,129,128]{2,1,0:T(8,128)S(1)} %get-tuple-element.3, f32[9,128,128]{2,1,0:T(8,128)S(1)} %copy-done.5), kind=kOutput, calls=%fused_computation.38 | convolution fusion | flops 3221225472 | bytes 16842752 | tf_op jit(solution)/shard_map/ijm,lm->ijl/dot_general | solution.py:52
  289.5 9.2 %fusion.34 = f32[128,128,128]{2,1,0:T(8,128)} fusion(f32[130,129,128]{2,1,0:T(8,128)S(1)} %get-tuple-element.3, f32[9,128,128]{2,1,0:T(8,128)S(1)} %copy-done.5), kind=kOutput, calls=%fused_computation.42 | convolution fusion | flops 3221225472 | bytes 16842752 | tf_op jit(solution)/shard_map/ijm,lm->ijl/dot_general | solution.py:52
  298.7 9.0 %fusion.32 = f32[128,128,128]{2,1,0:T(8,128)} fusion(f32[130,129,128]{2,1,0:T(8,128)S(1)} %get-tuple-element.2, f32[9,128,128]{2,1,0:T(8,128)S(1)} %copy-done.5), kind=kOutput, calls=%fused_computation.40 | convolution fusion | flops 3221225472 | bytes 16842752 | tf_op jit(solution)/shard_map/ijm,lm->ijl/dot_general | solution.py:52
  307.7 8.9 %fusion.36 = f32[128,128,128]{2,1,0:T(8,128)} fusion(f32[130,129,128]{2,1,0:T(8,128)S(1)} %get-tuple-element.2, f32[9,128,128]{2,1,0:T(8,128)S(1)} %copy-done.5), kind=kOutput, calls=%fused_computation.44 | convolution fusion | flops 3221225472 | bytes 16842752 | tf_op jit(solution)/shard_map/ijm,lm->ijl/dot_general | solution.py:52
  316.6 9.2 %fusion.38 = f32[128,128,128]{2,1,0:T(8,128)} fusion(f32[130,129,128]{2,1,0:T(8,128)S(1)} %get-tuple-element.3, f32[9,128,128]{2,1,0:T(8,128)S(1)} %copy-done.5), kind=kOutput, calls=%fused_computation.46 | convolution fusion | flops 3221225472 | bytes 16842752 | tf_op jit(solution)/shard_map/ijm,lm->ijl/dot_general | solution.py:52
  325.8 31.4 %add_add_fusion = f32[128,128,128]{2,1,0:T(8,128)} fusion(f32[128,128,128]{2,1,0:T(8,128)} %param.8, f32[128,128,128]{2,1,0:T(8,128)} %fusion.12, f32[128,128,128]{2,1,0:T(8,128)} %fusion.30, f32[128,128,128]{2,1,0:T(8,128)} %fusion.32, f32[128,128,128]{2,1,0:T(8,128)} %fusion.79, f32[128,128,128]{2,1,0:T(8,128)} %fusion.34, f32[128,128,128]{2,1,0:T(8,128)} %fusion.36, ...), kind=kOutput, calls=%fused_computation.54 | convolution fusion | flops 3240099840 | bytes 92340224 | tf_op jit(solution)/shard_map/ijm,lm->ijl/dot_general | solution.py:52
  (67 shorter events, 35.4 us)
Async XLA Ops:
  0.6 170.1 %copy-start = (f32[128,128]{1,0:T(8,128)S(1)}, f32[128,128]{1,0:T(8,128)}, u32[]{:S(2)}) copy-start(f32[128,128]{1,0:T(8,128)} %param.10) | copy-start | bytes 196612
  1.6 24.1 %collective-permute-start = (f32[1,128,128]{2,1,0:T(8,128)S(1)}, f32[1,128,128]{2,1,0:T(8,128)S(1)}, u32[]{:S(2)}, u32[]{:S(2)}) collective-permute-start(f32[1,128,128]{2,1,0:T(8,128)S(1)} %get-tuple-element.10), channel_id=1, source_target_pairs={{0,8},{8,16},{16,24},{1,9},{9,17},{17,25},{2,10},{10,18},{18,26},{... | collective-permute-start | bytes 196616 | tf_op jit(solution)/shard_map/ppermute | solution.py:20
  3.9 25.8 %collective-permute-start.1 = (f32[1,128,128]{2,1,0:T(8,128)S(1)}, f32[1,128,128]{2,1,0:T(8,128)S(1)}, u32[]{:S(2)}, u32[]{:S(2)}) collective-permute-start(f32[1,128,128]{2,1,0:T(8,128)S(1)} %get-tuple-element.11), channel_id=1, source_target_pairs={{8,0},{16,8},{24,16},{9,1},{17,9},{25,17},{10,2},{18,10},{26,18},{... | collective-permute-start | bytes 196616 | tf_op jit(solution)/shard_map/ppermute | solution.py:21
  5.2 165.5 %all-to-all-start = ((bf16[32,64,128]{2,1,0:T(8,128)(2,1)}), bf16[32,64,128]{2,1,0:T(8,128)(2,1)S(1)}, u32[]{:S(2)}, u32[]{:S(2)}) async-start(bf16[32,64,128]{2,1,0:T(8,128)(2,1)} %bitcast.95), calls=%async_computation | async-start | bytes 1048576 | tf_op jit(solution)/shard_map/all_to_all | solution.py:99
  14.5 10.9 %copy-start.6 = (s32[1,2048]{1,0:T(1,128)S(1)}, s32[1,2048]{1,0:T(1,128)}, u32[]{:S(2)}) copy-start(s32[1,2048]{1,0:T(1,128)} %param.13) | copy-start | bytes 24580
  14.5 10.9 %copy-start.7 = (f32[1,2,2048]{2,1,0:T(2,128)S(1)}, f32[1,2,2048]{2,1,0:T(2,128)}, u32[]{:S(2)}) copy-start(f32[1,2,2048]{2,1,0:T(2,128)} %param.14) | copy-start | bytes 49156
  14.5 11.0 %copy-start.8 = (s32[1,32]{1,0:T(1,128)S(1)}, s32[1,32]{1,0:T(1,128)}, u32[]{:S(2)}) copy-start(s32[1,32]{1,0:T(1,128)} %param.12) | copy-start | bytes 388
  25.7 10.5 %copy-start.4 = (f32[9,128,128]{2,1,0:T(8,128)S(1)}, f32[9,128,128]{2,1,0:T(8,128)}, u32[]{:S(2)}) copy-start(f32[9,128,128]{2,1,0:T(8,128)} %param.9) | copy-start | bytes 1769476
  29.7 65.0 %copy-start.2 = (f32[130,128,128]{2,1,0:T(8,128)}, f32[130,128,128]{2,1,0:T(8,128)S(1)}, u32[]{:S(2)}) copy-start(f32[130,128,128]{2,1,0:T(8,128)S(1)} %constant_dynamic-update-slice_fusion) | copy-start | bytes 25559044
  29.8 44.0 %collective-permute-start.3 = (f32[130,1,128]{2,1,0:T(1,128)S(1)}, f32[130,1,128]{2,1,0:T(1,128)S(1)}, u32[]{:S(2)}, u32[]{:S(2)}) collective-permute-start(f32[130,1,128]{2,1,0:T(1,128)S(1)} %get-tuple-element.6), channel_id=1, source_target_pairs={{1,0},{2,1},{3,2},{4,3},{5,4},{6,5},{7,6},{9,8},{10,9},{11,10},{12... | collective-permute-start | bytes 199688 | tf_op jit(solution)/shard_map/ppermute | solution.py:21
  31.1 15.9 %slice-start.2 = ((s8[8388608]{0:T(1024)(128)(4,1)}), s8[4194304]{0:T(1024)(128)(4,1)S(1)}, s32[]{:S(2)}) async-start(s8[8388608]{0:T(1024)(128)(4,1)} %bitcast.91), calls=%async_computation.4 | async-start | bytes 8388608
  31.2 15.9 %slice-start.3 = ((s8[8388608]{0:T(1024)(128)(4,1)}), s8[4194304]{0:T(1024)(128)(4,1)S(1)}, s32[]{:S(2)}) async-start(s8[8388608]{0:T(1024)(128)(4,1)} %bitcast.91), calls=%async_computation.5 | async-start | bytes 8388608
  31.2 24.8 %collective-permute-start.2 = (f32[130,1,128]{2,1,0:T(1,128)S(1)}, f32[130,1,128]{2,1,0:T(1,128)S(1)}, u32[]{:S(2)}, u32[]{:S(2)}) collective-permute-start(f32[130,1,128]{2,1,0:T(1,128)S(1)} %get-tuple-element.7), channel_id=1, source_target_pairs={{0,1},{1,2},{2,3},{3,4},{4,5},{5,6},{6,7},{8,9},{9,10},{10,11},{11... | collective-permute-start | bytes 199688 | tf_op jit(solution)/shard_map/ppermute | solution.py:20
  163.3 7.5 %copy-start.9 = (f32[1,2048]{1,0:T(1,128)S(1)}, f32[1,2048]{1,0:T(1,128)}, u32[]{:S(2)}) copy-start(f32[1,2048]{1,0:T(1,128)} %param.15) | copy-start | bytes 24580
  228.2 21.0 %collective-permute-start.5 = (f32[1,128,128]{2,1,0:T(8,128)S(1)}, f32[1,128,128]{2,1,0:T(8,128)S(1)}, u32[]{:S(2)}, u32[]{:S(2)}) collective-permute-start(f32[1,128,128]{2,1,0:T(8,128)S(1)} %get-tuple-element.8), channel_id=1, source_target_pairs={{8,0},{16,8},{24,16},{9,1},{17,9},{25,17},{10,2},{18,10},{26,18},{... | collective-permute-start | bytes 196616 | tf_op jit(solution)/shard_map/ppermute | solution.py:21
  229.5 19.7 %collective-permute-start.4 = (f32[1,128,128]{2,1,0:T(8,128)S(1)}, f32[1,128,128]{2,1,0:T(8,128)S(1)}, u32[]{:S(2)}, u32[]{:S(2)}) collective-permute-start(f32[1,128,128]{2,1,0:T(8,128)S(1)} %get-tuple-element.9), channel_id=1, source_target_pairs={{0,8},{8,16},{16,24},{1,9},{9,17},{17,25},{2,10},{10,18},{18,26},{... | collective-permute-start | bytes 196616 | tf_op jit(solution)/shard_map/ppermute | solution.py:20
  243.4 13.3 %copy-start.5 = (f32[9,128,128]{2,1,0:T(8,128)S(1)}, f32[9,128,128]{2,1,0:T(8,128)}, u32[]{:S(2)}) copy-start(f32[9,128,128]{2,1,0:T(8,128)} %param.9) | copy-start | bytes 1769476
  243.4 113.8 %all-to-all-start.1 = ((bf16[32,64,128]{2,1,0:T(8,128)(2,1)}), bf16[32,64,128]{2,1,0:T(8,128)(2,1)S(1)}, u32[]{:S(2)}, u32[]{:S(2)}) async-start(bf16[32,64,128]{2,1,0:T(8,128)(2,1)} %bitcast.34), calls=%async_computation.1 | async-start | bytes 1048576 | tf_op jit(solution)/shard_map/all_to_all | solution.py:110
  250.5 26.1 %collective-permute-start.6 = (f32[130,1,128]{2,1,0:T(1,128)S(1)}, f32[130,1,128]{2,1,0:T(1,128)S(1)}, u32[]{:S(2)}, u32[]{:S(2)}) collective-permute-start(f32[130,1,128]{2,1,0:T(1,128)S(1)} %get-tuple-element.5), channel_id=1, source_target_pairs={{1,0},{2,1},{3,2},{4,3},{5,4},{6,5},{7,6},{9,8},{10,9},{11,10},{12... | collective-permute-start | bytes 199688 | tf_op jit(solution)/shard_map/ppermute | solution.py:21
  251.8 15.9 %slice-start = ((s8[8388608]{0:T(1024)(128)(4,1)}), s8[4194304]{0:T(1024)(128)(4,1)S(1)}, s32[]{:S(2)}) async-start(s8[8388608]{0:T(1024)(128)(4,1)} %bitcast.87), calls=%async_computation.2 | async-start | bytes 8388608
  251.8 15.9 %slice-start.1 = ((s8[8388608]{0:T(1024)(128)(4,1)}), s8[4194304]{0:T(1024)(128)(4,1)S(1)}, s32[]{:S(2)}) async-start(s8[8388608]{0:T(1024)(128)(4,1)} %bitcast.87), calls=%async_computation.3 | async-start | bytes 8388608
  251.9 24.8 %collective-permute-start.7 = (f32[130,1,128]{2,1,0:T(1,128)S(1)}, f32[130,1,128]{2,1,0:T(1,128)S(1)}, u32[]{:S(2)}, u32[]{:S(2)}) collective-permute-start(f32[130,1,128]{2,1,0:T(1,128)S(1)} %get-tuple-element.4), channel_id=1, source_target_pairs={{0,1},{1,2},{2,3},{3,4},{4,5},{5,6},{6,7},{8,9},{9,10},{10,11},{11... | collective-permute-start | bytes 199688 | tf_op jit(solution)/shard_map/ppermute | solution.py:20
  280.5 27.1 %copy-start.3 = (f32[130,129,128]{2,1,0:T(8,128)}, f32[130,129,128]{2,1,0:T(8,128)S(1)}, u32[]{:S(2)}) copy-start(f32[130,129,128]{2,1,0:T(8,128)S(1)} %get-tuple-element.2) | copy-start | bytes 25758724
  325.8 32.2 %copy-start.1 = (f32[128,128]{1,0:T(8,128)S(1)}, f32[128,128]{1,0:T(8,128)}, u32[]{:S(2)}) copy-start(f32[128,128]{1,0:T(8,128)} %param.10) | copy-start | bytes 196612
where the time goes:
time: 363 us; the launch traced here: 359 us
  matrix products  222 us (61%)
  other arithmetic  61.2 us (17%)
  local copies, waits for them, and re-layouts  38 us (10%)
  starting transfers between devices  35.4 us (10%)
    dot_general x9, matrix products, transpose_summed(): jnp.einsum('ijm,lm->ijl', piece, corr_blocks[which], precision=lax.Precis...  107 us
    dot_general x9, matrix products, root_summed(): jnp.einsum('ijl,lm->ijm', piece, corr_blocks[which], precision=lax.Precis...  107 us
    scatter-add x1, other arithmetic, observe(): jax.ops.segment_sum(spread_terms, targets, num_segments=state_rows.shape[0])  48.4 us
    gather x1, local copies, waits for them, and re-layouts, observe(): picked = jnp.take(state_rows, targets, axis=0)  31.1 us
    ppermute x4, starting transfers between devices, with_halo(): before = lax.ppermute(last, axis, up)  15.2 us
    all_to_all x1, starting transfers between devices, body(): lax.all_to_all(outgoing, ('lat', 'lon'), split_axis=0, concat_axis=0, til...  9.21 us
    select_n x2, other arithmetic, observe(): picked = jnp.take(state_rows, targets, axis=0)  7.49 us
  transfers between devices with their start and end apart: 10, of which 0 were waited for; matrix products, arithmetic and copies ran while one was open for 73% of the time, Pallas kernels for 0%

commit v1 on v0

v1 whole, which is shorter than its diff:
```python
import functools
import jax
import jax.numpy as jnp
from jax import lax
from jax.experimental import pallas as pl
from jax.experimental.pallas import tpu as pltpu
from jax.sharding import PartitionSpec as P

CAP = 64
CS = 128
EDGE = 8
F32 = jnp.float32
BF16 = jnp.bfloat16
UNROLL = 8


def split(x):
    hi = x.astype(BF16)
    return hi, (x - hi.astype(F32)).astype(BF16)


def column(row):
    return jnp.broadcast_to(row, (128, CS)).T


def combined(corr_ref, jac_ref, k):
    return jnp.dot(corr_ref[k], jac_ref[...], precision=lax.Precision.HIGHEST, preferred_element_type=F32)


def forward_kernel(pitch, col_ref, frac_ref, corr_ref, jac_ref, north_ref, south_ref, west_ref, east_ref, control_ref,
                   out_ref, pad, planes, p_hi, p_lo, g_both, sem):
    rows, cols, _ = control_ref.shape
    fetch = pltpu.make_async_copy(control_ref, pad.at[pl.ds(1, rows), pl.ds(EDGE, cols), :], sem)
    fetch.start()
    for k in range(9):
        hi, lo = split(combined(corr_ref, jac_ref, k))
        g_both[k * 128:(k + 1) * 128, 0:128] = hi
        g_both[k * 128:(k + 1) * 128, 128:256] = lo
    pad[0, EDGE:EDGE + cols, :] = north_ref[...]
    pad[rows + 1, EDGE:EDGE + cols, :] = south_ref[...]
    for side, at in ((west_ref, EDGE - 1), (east_ref, EDGE + cols)):
        def put(i, c, side=side, at=at):
            pad[pl.ds(i, 1), at:at + 1, :] = side[pl.ds(i, 1), :].reshape(1, 1, 128)
            return c
        lax.fori_loop(0, rows + 2, put, 0)
    fetch.wait()
    flat = pad.reshape((rows + 2) * pitch, 128)

    def chunk(n, carry):
        first = n * CS

        def pick(t, c):
            for v in range(UNROLL):
                s = t * UNROLL + v
                corner = col_ref[0, first + s]
                base = corner + (corner // cols) * (pitch - cols) + (EDGE - 1)
                for r in range(4):
                    planes[pl.ds(r * 4 * CS + s, 4, stride=CS), :] = flat[pl.ds(base + r * pitch, 4), :]
            return c

        lax.fori_loop(0, CS // UNROLL, pick, 0)
        at = pl.ds(pl.multiple_of(first, CS), CS)
        f = column(frac_ref[0, 0:1, at])
        g = column(frac_ref[0, 1:2, at])
        for a in range(3):
            lat = []
            for q in range(4):
                low = planes[(a * 4 + q) * CS:(a * 4 + q + 1) * CS, :]
                high = planes[((a + 1) * 4 + q) * CS:((a + 1) * 4 + q + 1) * CS, :]
                lat.append((1.0 - f) * low + f * high)
            for b in range(3):
                hi, lo = split((1.0 - g) * lat[b] + g * lat[b + 1])
                k = 3 * a + b
                p_hi[:, k * 128:(k + 1) * 128] = hi
                p_lo[:, k * 128:(k + 1) * 128] = lo
        both = jnp.dot(p_hi[...], g_both[...], preferred_element_type=F32)
        both += jnp.dot(p_lo[...], g_both[...], preferred_element_type=F32)
        out_ref[at, :] = both[:, 0:128] + both[:, 128:256]
        return carry

    lax.fori_loop(0, col_ref.shape[1] // CS, chunk, 0)


def adjoint_kernel(pitch, col_ref, frac_ref, corr_ref, jac_ref, weighted_ref, control_ref,
                   grad_ref, north_ref, south_ref, west_ref, east_ref, pad, planes, q_ref, gt_hi, gt_lo, sem):
    rows, cols, _ = control_ref.shape
    inner = pad.at[pl.ds(1, rows), pl.ds(EDGE, cols), :]
    fetch = pltpu.make_async_copy(control_ref, inner, sem)
    fetch.start()
    for k in range(9):
        hi, lo = split(combined(corr_ref, jac_ref, k).T)
        for half in range(2):
            gt_hi[half * 128:(half + 1) * 128, k * 128:(k + 1) * 128] = hi
            gt_lo[half * 128:(half + 1) * 128, k * 128:(k + 1) * 128] = lo
    for i in (0, rows + 1):
        pad[i] = jnp.zeros((pitch, 128), F32)

    def clear(i, c):
        pad[pl.ds(i, 1), 0:EDGE, :] = jnp.zeros((1, EDGE, 128), F32)
        pad[pl.ds(i, 1), EDGE + cols:pitch, :] = jnp.zeros((1, pitch - cols - EDGE, 128), F32)
        return c

    lax.fori_loop(1, rows + 1, clear, 0)
    fetch.wait()
    flat = pad.reshape((rows + 2) * pitch, 128)

    def chunk(n, carry):
        first = n * CS
        at = pl.ds(pl.multiple_of(first, CS), CS)
        w_hi, w_lo = split(weighted_ref[at, :])
        w = jnp.concatenate([w_hi, w_lo], axis=1)
        q_ref[...] = (jnp.dot(w, gt_hi[...], preferred_element_type=F32)
                      + jnp.dot(w, gt_lo[...], preferred_element_type=F32))
        f = column(frac_ref[0, 0:1, at])
        g = column(frac_ref[0, 1:2, at])
        for c in range(4):
            line = []
            for a in range(3):
                part = None
                if c < 3:
                    part = (1.0 - g) * q_ref[:, (3 * a + c) * 128:(3 * a + c + 1) * 128]
                if c > 0:
                    other = g * q_ref[:, (3 * a + c - 1) * 128:(3 * a + c) * 128]
                    part = other if part is None else part + other
                line.append(part)
            for r in range(4):
                part = None
                if r < 3:
                    part = (1.0 - f) * line[r]
                if r > 0:
                    other = f * line[r - 1]
                    part = other if part is None else part + other
                planes[(r * 4 + c) * CS:(r * 4 + c + 1) * CS, :] = part

        def spread(t, c):
            for v in range(UNROLL):
                s = t * UNROLL + v
                corner = col_ref[0, first + s]
                base = corner + (corner // cols) * (pitch - cols) + (EDGE - 1)
                for r in range(4):
                    flat[pl.ds(base + r * pitch, 4), :] += planes[pl.ds(r * 4 * CS + s, 4, stride=CS), :]
            return c

        lax.fori_loop(0, CS // UNROLL, spread, 0)
        return carry

    lax.fori_loop(0, col_ref.shape[1] // CS, chunk, 0)
    send = pltpu.make_async_copy(inner, grad_ref, sem)
    send.start()
    north_ref[...] = pad[0]
    south_ref[...] = pad[rows + 1]
    west_ref[...] = flat[pl.ds(pitch + EDGE - 1, rows, stride=pitch), :]
    east_ref[...] = flat[pl.ds(pitch + EDGE + cols, rows, stride=pitch), :]
    send.wait()


def finish_kernel(north_ref, south_ref, west_ref, east_ref, nw_ref, ne_ref, sw_ref, se_ref, grad_in,
                  grad_ref, line_n, line_s, tile_w, tile_e, sems):
    rows, cols, _ = grad_in.shape
    inner = pl.ds(1, rows - 2)
    ends = ((grad_ref.at[0], line_n), (grad_ref.at[rows - 1], line_s),
            (grad_ref.at[inner, pl.ds(0, 8), :], tile_w), (grad_ref.at[inner, pl.ds(cols - 8, 8), :], tile_e))
    loads = [pltpu.make_async_copy(far, near, sems.at[i]) for i, (far, near) in enumerate(ends)]
    for copy in loads:
        copy.start()
    for copy in loads:
        copy.wait()
    line_n[...] += north_ref[...]
    line_s[...] += south_ref[...]
    line_n[0:1, :] += west_ref[0:1, :] + nw_ref[...]
    line_n[cols - 1:cols, :] += east_ref[0:1, :] + ne_ref[...]
    line_s[0:1, :] += west_ref[rows - 1:rows, :] + sw_ref[...]
    line_s[cols - 1:cols, :] += east_ref[rows - 1:rows, :] + se_ref[...]

    flat_w = tile_w.reshape((rows - 2) * 8, 128)
    flat_e = tile_e.reshape((rows - 2) * 8, 128)
    flat_w[pl.ds(0, rows - 2, stride=8), :] += west_ref[1:rows - 1, :]
    flat_e[pl.ds(7, rows - 2, stride=8), :] += east_ref[1:rows - 1, :]
    stores = [pltpu.make_async_copy(near, far, sems.at[i]) for i, (far, near) in enumerate(ends)]
    for copy in stores:
        copy.start()
    for copy in stores:
        copy.wait()


def shift(x, d_lat, d_lon):
    n_lat, n_lon = lax.axis_size("lat"), lax.axis_size("lon")
    pairs = []
    for p in range(n_lat):
        for q in range(n_lon):
            to_p, to_q = p + d_lat, q + d_lon
            if 0 <= to_p < n_lat and 0 <= to_q < n_lon:
                pairs.append((p * n_lon + q, to_p * n_lon + to_q))
    return lax.ppermute(x, ("lat", "lon"), pairs)


def body(control, corr_blocks, jacobian, obs_values, obs_count, obs_col, obs_frac, obs_rinv):
    n_devices = lax.axis_size("lat") * lax.axis_size("lon")
    rows, cols, levels = control.shape
    channels = jacobian.shape[1]
    slots = obs_col.shape[1]
    pitch = cols + 2 * EDGE
    vmem = pl.BlockSpec(memory_space=pltpu.VMEM)
    smem = pl.BlockSpec(memory_space=pltpu.SMEM)
    hbm = pl.BlockSpec(memory_space=pl.ANY)

    incoming = lax.all_to_all(obs_values.reshape(n_devices, CAP, channels), ("lat", "lon"),
                              split_axis=0, concat_axis=0, tiled=True)
    north = shift(control[rows - 1], 1, 0)
    south = shift(control[0], -1, 0)
    west = shift(control[:, cols - 1], 0, 1)
    east = shift(control[:, 0], 0, -1)
    nw = shift(control[rows - 1, cols - 1:], 1, 1)
    ne = shift(control[rows - 1, :1], 1, -1)
    sw = shift(control[0, cols - 1:], -1, 1)
    se = shift(control[0, :1], -1, -1)
    west = jnp.concatenate([nw, west, sw])
    east = jnp.concatenate([ne, east, se])

    limit = pltpu.CompilerParams(vmem_limit_bytes=40 * 2**20)
    evolved = pl.pallas_call(
        functools.partial(forward_kernel, pitch),
        out_shape=jax.ShapeDtypeStruct((slots, channels), F32),
        in_specs=[smem] + [vmem] * 7 + [hbm],
        out_specs=vmem,
        scratch_shapes=[
            pltpu.VMEM((rows + 2, pitch, levels), F32),
            pltpu.VMEM((16 * CS, levels), F32),
            pltpu.VMEM((CS, 9 * levels), BF16),
            pltpu.VMEM((CS, 9 * levels), BF16),
            pltpu.VMEM((9 * levels, 2 * channels), BF16),
            pltpu.SemaphoreType.DMA,
        ],
        compiler_params=limit,
        cost_estimate=pl.CostEstimate(flops=2 * slots * 1152 * 512, bytes_accessed=40 * 2**20, transcendentals=0),
        name="forward",
    )(obs_col, obs_frac, corr_blocks, jacobian, north, south, west, east, control)

    departure = evolved - incoming.reshape(slots, channels).astype(F32)
    live = (jnp.arange(CAP, dtype=jnp.int32)[None, :] < obs_count[0][:, None]).reshape(slots, 1)
    weighted = jnp.where(live, obs_rinv[0][:, None] * departure, jnp.zeros_like(departure))
    returned = lax.all_to_all(weighted.astype(BF16).reshape(n_devices, CAP, channels), ("lat", "lon"),
                              split_axis=0, concat_axis=0, tiled=True)

    gradient, out_n, out_s, out_w, out_e = pl.pallas_call(
        functools.partial(adjoint_kernel, pitch),
        out_shape=[
            jax.ShapeDtypeStruct(control.shape, F32),
            jax.ShapeDtypeStruct((pitch, levels), F32),
            jax.ShapeDtypeStruct((pitch, levels), F32),
            jax.ShapeDtypeStruct((rows, levels), F32),
            jax.ShapeDtypeStruct((rows, levels), F32),
        ],
        in_specs=[smem] + [vmem] * 4 + [hbm],
        out_specs=[hbm] + [vmem] * 4,
        scratch_shapes=[
            pltpu.VMEM((rows + 2, pitch, levels), F32),
            pltpu.VMEM((16 * CS, levels), F32),
            pltpu.VMEM((CS, 9 * levels), F32),
            pltpu.VMEM((2 * channels, 9 * levels), BF16),
            pltpu.VMEM((2 * channels, 9 * levels), BF16),
            pltpu.SemaphoreType.DMA,
        ],
        compiler_params=limit,
        cost_estimate=pl.CostEstimate(flops=2 * slots * 1152 * 512, bytes_accessed=60 * 2**20, transcendentals=0),
        name="adjoint",
    )(obs_col, obs_frac, corr_blocks, jacobian, weighted, control)

    got_s = shift(out_n[EDGE:EDGE + cols], -1, 0)
    got_n = shift(out_s[EDGE:EDGE + cols], 1, 0)
    got_e = shift(out_w, 0, -1)
    got_w = shift(out_e, 0, 1)
    got_se = shift(out_n[EDGE - 1:EDGE], -1, -1)
    got_sw = shift(out_n[EDGE + cols:EDGE + cols + 1], -1, 1)
    got_ne = shift(out_s[EDGE - 1:EDGE], 1, -1)
    got_nw = shift(out_s[EDGE + cols:EDGE + cols + 1], 1, 1)
    gradient = pl.pallas_call(
        finish_kernel,
        out_shape=jax.ShapeDtypeStruct(control.shape, F32),
        in_specs=[vmem] * 8 + [hbm],
        out_specs=hbm,
        scratch_shapes=[
            pltpu.VMEM((cols, levels), F32),
            pltpu.VMEM((cols, levels), F32),
            pltpu.VMEM((rows - 2, 8, levels), F32),
            pltpu.VMEM((rows - 2, 8, levels), F32),
            pltpu.SemaphoreType.DMA((4,)),
        ],
        input_output_aliases={8: 0},
        name="finish",
    )(got_n, got_s, got_w, got_e, got_nw, got_ne, got_sw, got_se, gradient)
    return (gradient, returned.reshape(n_devices * CAP, channels))


def solution(mesh):
    in_specs = (
        P("lat", "lon", None),
        P(),
        P(),
        P(("lat", "lon"), None),
        P(("lat", "lon"), None),
        P(("lat", "lon"), None),
        P(("lat", "lon"), None, None),
        P(("lat", "lon"), None),
    )
    out_specs = (P("lat", "lon", None), P(("lat", "lon"), None))
    return jax.shard_map(body, mesh=mesh, in_specs=in_specs, out_specs=out_specs, check_vma=False)
```

time: 363 us -> 155 us (0.43)
  matrix products: 222 us -> 0 us
  Pallas kernels: 0 us -> 68.6 us
  other arithmetic: 61.2 us -> 2.23 us
  starting transfers between devices: 35.4 us -> 60.3 us
  local copies, waits for them, and re-layouts: 38 us -> 14.6 us
  waiting for transfers between devices: 0.03 us -> 6.19 us
    dot_general x20 -> x0, matrix products: 222 us -> none  [the longest x9 107 us: transpose_summed(): jnp.einsum('ijm,lm->ijl', piece, corr_blocks[which], precision=lax.Precis...]
    pallas_call x0 -> x3, Pallas kernels: none -> 68.6 us  [the longest x1 34.5 us: body(): pl.pallas_call(functools.partial(forward_kernel, pitch), out_shape=jax.Sh...]
    scatter-add x1 -> x0, other arithmetic: 48.4 us -> none  [observe(): jax.ops.segment_sum(spread_terms, targets, num_segments=state_rows.shape[0])]
    gather x1 -> x0, local copies, waits for them, and re-layouts: 31.1 us -> none  [observe(): picked = jnp.take(state_rows, targets, axis=0)]
    ppermute x8 -> x16, starting transfers between devices: 20.4 us -> 47.7 us  [shift(): return lax.ppermute(x, ('lat', 'lon'), pairs)]
    select_n x2 -> x0, other arithmetic: 7.49 us -> none  [observe(): picked = jnp.take(state_rows, targets, axis=0)]
    unnamed x31 -> x39, local copies, waits for them, and re-layouts: 4.91 us -> 11.5 us
    ppermute x8 -> x16, waiting for transfers between devices: 0.02 us -> 6.19 us  [shift(): return lax.ppermute(x, ('lat', 'lon'), pairs)]
  transfers between devices with their start and end apart: 10 -> 18, of which waited for: 0 -> 2; matrix products, arithmetic and copies ran while one was open for 73% -> 2% of each run, Pallas kernels for 0% -> 45%
where the time goes in v1:
time: 155 us; the launch traced here: 153 us
  Pallas kernels  68.6 us (44%)
  starting transfers between devices  60.3 us (39%)
  local copies, waits for them, and re-layouts  14.6 us (9%)
  waiting for transfers between devices  6.19 us (4%)
  other arithmetic  2.23 us (1%)
    ppermute x16, starting transfers between devices, shift(): return lax.ppermute(x, ('lat', 'lon'), pairs)  47.7 us
    pallas_call x1, Pallas kernels, body(): pl.pallas_call(functools.partial(forward_kernel, pitch), out_shape=jax.Sh...  34.5 us
    pallas_call x1, Pallas kernels, body(): pl.pallas_call(functools.partial(adjoint_kernel, pitch), out_shape=[jax.S...  30.9 us
    unnamed x39, local copies, waits for them, and re-layouts  11.5 us
    all_to_all x1, starting transfers between devices, body(): lax.all_to_all(obs_values.reshape(n_devices, CAP, channels), ('lat', 'lon...  7.3 us
    ppermute x16, waiting for transfers between devices, shift(): return lax.ppermute(x, ('lat', 'lon'), pairs)  6.19 us
    all_to_all x1, starting transfers between devices, body(): lax.all_to_all(weighted.astype(BF16).reshape(n_devices, CAP, channels), (...  5.28 us
    pallas_call x1, Pallas kernels, body(): pl.pallas_call(finish_kernel, out_shape=jax.ShapeDtypeStruct(control.shap...  3.27 us
  transfers between devices with their start and end apart: 18, of which 2 were waited for; matrix products, arithmetic and copies ran while one was open for 2% of the time, Pallas kernels for 45%

profile of v1, /device:TPU:0, one launch (start us, length us, event | category | flops | bytes accessed | tf_op | source)
XLA Modules:
  0.0 153.0 jit_solution(12797635137818510289)
XLA Ops:
  0.7 7.3 %all-to-all-start = ((bf16[32,64,128]{2,1,0:T(8,128)(2,1)}), bf16[32,64,128]{2,1,0:T(8,128)(2,1)S(1)}, u32[]{:S(2)}, u32[]{:S(2)}) async-start(bf16[32,64,128]{2,1,0:T(8,128)(2,1)} %bitcast.29), calls=%async_computation | async-start | bytes 1048576 | tf_op jit(solution)/shard_map/all_to_all | solution.py:207
  9.4 1.3 collective-permute-start.7
  11.4 8.6 %collective-permute-start.2 = (f32[1,128]{1,0:T(1,128)S(1)}, f32[1,128]{1,0:T(1,128)S(1)}, u32[]{:S(2)}, u32[]{:S(2)}) collective-permute-start(f32[1,128]{1,0:T(1,128)S(1)} %get-tuple-element.17), channel_id=1, source_target_pairs={{0,9},{1,10},{2,11},{3,12},{4,13},{5,14},{6,15},{8,17},{9,18},{10,... | collective-permute-start | bytes 1544 | tf_op jit(solution)/shard_map/ppermute | solution.py:194
  19.9 1.3 fusion.4
  21.2 3.7 %collective-permute-start.3 = (f32[128,128]{1,0:T(8,128)S(1)}, f32[128,128]{1,0:T(8,128)S(1)}, u32[]{:S(2)}, u32[]{:S(2)}) collective-permute-start(f32[128,128]{1,0:T(8,128)S(1)} %bitcast.31), channel_id=1, source_target_pairs={{0,1},{1,2},{2,3},{3,4},{4,5},{5,6},{6,7},{8,9},{9,10},{10,11},{11... | collective-permute-start | bytes 196616 | tf_op jit(solution)/shard_map/ppermute | solution.py:194
  26.7 1.3 collective-permute-start.1
  28.0 4.1 %collective-permute-start = (f32[128,128]{1,0:T(8,128)S(1)}, f32[128,128]{1,0:T(8,128)S(1)}, u32[]{:S(2)}, u32[]{:S(2)}) collective-permute-start(f32[128,128]{1,0:T(8,128)S(1)} %get-tuple-element.21), channel_id=1, source_target_pairs={{0,8},{1,9},{2,10},{3,11},{4,12},{5,13},{6,14},{7,15},{8,16},{9,17... | collective-permute-start | bytes 196616 | tf_op jit(solution)/shard_map/ppermute | solution.py:194
  32.1 1.3 collective-permute-start.6
  33.4 4.9 %collective-permute-done.6 = f32[128,128]{1,0:T(8,128)S(1)} collective-permute-done((f32[128,128]{1,0:T(8,128)S(1)}, f32[128,128]{1,0:T(8,128)S(1)}, u32[]{:S(2)}, u32[]{:S(2)}) %collective-permute-start.6) | collective-permute-done | bytes 65568 | tf_op jit(solution)/shard_map/ppermute | solution.py:194
  38.4 3.4 %copy-done = f32[128,128,128]{2,1,0:T(8,128)S(1)} copy-done((f32[128,128,128]{2,1,0:T(8,128)S(1)}, f32[128,128,128]{2,1,0:T(8,128)}, u32[]{:S(2)}) %copy-start) | copy-done | bytes 8388632
  41.7 1.1 copy-done.2
  45.1 34.5 %forward.1 = f32[2048,128]{1,0:T(8,128)S(1)} custom-call(s32[1,2048]{1,0:T(1,128)S(1)} %copy-done.8, f32[1,2,2048]{2,1,0:T(2,128)S(1)} %copy-done.6, f32[9,128,128]{2,1,0:T(8,128)S(1)} %copy-done.2, f32[128,128]{1,0:T(8,128)S(1)} %copy-done.4, f32[128,128]{1,0:T(8,128)S(1)} %collective-permute-done.north_ref, ...), custom_call_target="tpu_custom_call" | custom-call | flops 2415919104 | bytes 41943040 | tf_op jit(solution)/shard_map/forward/pallas_call | solution.py:221
  79.5 1.5 fusion.2
  81.0 5.3 %all-to-all-start.1 = ((bf16[32,64,128]{2,1,0:T(8,128)(2,1)}), bf16[32,64,128]{2,1,0:T(8,128)(2,1)S(1)}, u32[]{:S(2)}, u32[]{:S(2)}) async-start(bf16[32,64,128]{2,1,0:T(8,128)(2,1)} %bitcast.28), calls=%async_computation.1 | async-start | bytes 1048576 | tf_op jit(solution)/shard_map/all_to_all | solution.py:242
  86.4 3.4 %copy-done.1 = f32[128,128,128]{2,1,0:T(8,128)S(1)} copy-done((f32[128,128,128]{2,1,0:T(8,128)S(1)}, f32[128,128,128]{2,1,0:T(8,128)}, u32[]{:S(2)}) %copy-start.1) | copy-done | bytes 8388632
  89.7 30.9 %adjoint.1 = (f32[128,128,128]{2,1,0:T(8,128)}, f32[144,128]{1,0:T(8,128)S(1)}, f32[144,128]{1,0:T(8,128)S(1)}, f32[128,128]{1,0:T(8,128)S(1)}, f32[128,128]{1,0:T(8,128)S(1)}) custom-call(s32[1,2048]{1,0:T(1,128)S(1)} %copy-done.9, f32[1,2,2048]{2,1,0:T(2,128)S(1)} %copy-done.7, f32[9,128,128]{2,1,0:T(8,128)S(1)} %copy-done.3, f32[128,128]{1,0:T(8,128)S(1)} %copy-done.5, ...), custom_call_target="tpu_custom_call" | custom-call | flops 2415919104 | bytes 62914560 | tf_op jit(solution)/shard_map/adjoint/pallas_call | solution.py:245
  120.7 1.3 collective-permute-start.15
  122.7 1.3 collective-permute-start.9
  124.0 5.7 %collective-permute-start.8 = (f32[128,128]{1,0:T(8,128)S(1)}, f32[128,128]{1,0:T(8,128)S(1)}, u32[]{:S(2)}, u32[]{:S(2)}) collective-permute-start(f32[128,128]{1,0:T(8,128)S(1)} %slice.50), channel_id=1, source_target_pairs={{0,8},{1,9},{2,10},{3,11},{4,12},{5,13},{6,14},{7,15},{8,16},{9,17... | collective-permute-start | bytes 196616 | tf_op jit(solution)/shard_map/ppermute | solution.py:194
  129.6 3.4 %collective-permute-start.10 = (f32[128,128]{1,0:T(8,128)S(1)}, f32[128,128]{1,0:T(8,128)S(1)}, u32[]{:S(2)}, u32[]{:S(2)}) collective-permute-start(f32[128,128]{1,0:T(8,128)S(1)} %get-tuple-element.9), channel_id=1, source_target_pairs={{0,1},{1,2},{2,3},{3,4},{4,5},{5,6},{6,7},{8,9},{9,10},{10,11},{11... | collective-permute-start | bytes 196616 | tf_op jit(solution)/shard_map/ppermute | solution.py:194
  133.0 1.3 collective-permute-start.11
  135.1 11.9 %collective-permute-start.12 = (f32[1,128]{1,0:T(1,128)S(1)}, f32[1,128]{1,0:T(1,128)S(1)}, u32[]{:S(2)}, u32[]{:S(2)}) collective-permute-start(f32[1,128]{1,0:T(1,128)S(1)} %get-tuple-element.25), channel_id=1, source_target_pairs={{0,9},{1,10},{2,11},{3,12},{4,13},{5,14},{6,15},{8,17},{9,18},{10,... | collective-permute-start | bytes 1544 | tf_op jit(solution)/shard_map/ppermute | solution.py:194
  147.0 1.3 collective-permute-done.12.nw_ref
  149.0 3.3 %finish.1 = f32[128,128,128]{2,1,0:T(8,128)} custom-call(f32[128,128]{1,0:T(8,128)} %copy-done.11, f32[128,128]{1,0:T(8,128)} %copy-done.10, f32[128,128]{1,0:T(8,128)} %copy-done.12, f32[128,128]{1,0:T(8,128)} %copy-done.13, f32[1,128]{1,0:T(1,128)} %copy-done.18, f32[1,128]{1,0:T(1,128)} %copy-done.17, ...), custom_call_target="tpu_custom_call", output_to_operand_aliasing={{}: (8, {})} | custom-call | tf_op jit(solution)/shard_map/finish/pallas_call | solution.py:277
  (66 shorter events, 8.9 us)
Async XLA Ops:
  0.6 85.7 %copy-start.7 = (f32[1,2,2048]{2,1,0:T(2,128)S(1)}, f32[1,2,2048]{2,1,0:T(2,128)}, u32[]{:S(2)}) copy-start(f32[1,2,2048]{2,1,0:T(2,128)} %frac_ref.3) | copy-start | bytes 49156
  0.6 85.7 %copy-start.9 = (s32[1,2048]{1,0:T(1,128)S(1)}, s32[1,2048]{1,0:T(1,128)}, u32[]{:S(2)}) copy-start(s32[1,2048]{1,0:T(1,128)} %col_ref.3) | copy-start | bytes 24580
  0.7 85.7 %copy-start.5 = (f32[128,128]{1,0:T(8,128)S(1)}, f32[128,128]{1,0:T(8,128)}, u32[]{:S(2)}) copy-start(f32[128,128]{1,0:T(8,128)} %jac_ref.3) | copy-start | bytes 196612
  0.7 85.7 %copy-start.3 = (f32[9,128,128]{2,1,0:T(8,128)S(1)}, f32[9,128,128]{2,1,0:T(8,128)}, u32[]{:S(2)}) copy-start(f32[9,128,128]{2,1,0:T(8,128)} %corr_ref.3) | copy-start | bytes 1769476
  0.7 78.9 %copy-start.14 = (f32[1,2048]{1,0:T(1,128)S(1)}, f32[1,2048]{1,0:T(1,128)}, u32[]{:S(2)}) copy-start(f32[1,2048]{1,0:T(1,128)} %param.15) | copy-start | bytes 24580
  0.7 78.8 %all-to-all-start = ((bf16[32,64,128]{2,1,0:T(8,128)(2,1)}), bf16[32,64,128]{2,1,0:T(8,128)(2,1)S(1)}, u32[]{:S(2)}, u32[]{:S(2)}) async-start(bf16[32,64,128]{2,1,0:T(8,128)(2,1)} %bitcast.29), calls=%async_computation | async-start | bytes 1048576 | tf_op jit(solution)/shard_map/all_to_all | solution.py:207
  8.7 24.7 %collective-permute-start.5 = (f32[1,128]{1,0:T(1,128)S(1)}, f32[1,128]{1,0:T(1,128)S(1)}, u32[]{:S(2)}, u32[]{:S(2)}) collective-permute-start(f32[1,128]{1,0:T(1,128)S(1)} %get-tuple-element.14), channel_id=1, source_target_pairs={{1,8},{2,9},{3,10},{4,11},{5,12},{6,13},{7,14},{9,16},{10,17},{11,... | collective-permute-start | bytes 1544 | tf_op jit(solution)/shard_map/ppermute | solution.py:194
  9.4 24.0 %collective-permute-start.7 = (f32[1,128]{1,0:T(1,128)S(1)}, f32[1,128]{1,0:T(1,128)S(1)}, u32[]{:S(2)}, u32[]{:S(2)}) collective-permute-start(f32[1,128]{1,0:T(1,128)S(1)} %get-tuple-element.15), channel_id=1, source_target_pairs={{9,0},{10,1},{11,2},{12,3},{13,4},{14,5},{15,6},{17,8},{18,9},{19,... | collective-permute-start | bytes 1544 | tf_op jit(solution)/shard_map/ppermute | solution.py:194
  10.7 16.0 %collective-permute-start.4 = (f32[1,128]{1,0:T(1,128)S(1)}, f32[1,128]{1,0:T(1,128)S(1)}, u32[]{:S(2)}, u32[]{:S(2)}) collective-permute-start(f32[1,128]{1,0:T(1,128)S(1)} %get-tuple-element.16), channel_id=1, source_target_pairs={{8,1},{9,2},{10,3},{11,4},{12,5},{13,6},{14,7},{16,9},{17,10},{18,... | collective-permute-start | bytes 1544 | tf_op jit(solution)/shard_map/ppermute | solution.py:194
  11.4 16.6 %collective-permute-start.2 = (f32[1,128]{1,0:T(1,128)S(1)}, f32[1,128]{1,0:T(1,128)S(1)}, u32[]{:S(2)}, u32[]{:S(2)}) collective-permute-start(f32[1,128]{1,0:T(1,128)S(1)} %get-tuple-element.17), channel_id=1, source_target_pairs={{0,9},{1,10},{2,11},{3,12},{4,13},{5,14},{6,15},{8,17},{9,18},{10,... | collective-permute-start | bytes 1544 | tf_op jit(solution)/shard_map/ppermute | solution.py:194
  21.2 10.9 %collective-permute-start.3 = (f32[128,128]{1,0:T(8,128)S(1)}, f32[128,128]{1,0:T(8,128)S(1)}, u32[]{:S(2)}, u32[]{:S(2)}) collective-permute-start(f32[128,128]{1,0:T(8,128)S(1)} %bitcast.31), channel_id=1, source_target_pairs={{0,1},{1,2},{2,3},{3,4},{4,5},{5,6},{6,7},{8,9},{9,10},{10,11},{11... | collective-permute-start | bytes 196616 | tf_op jit(solution)/shard_map/ppermute | solution.py:194
  26.7 11.7 %collective-permute-start.1 = (f32[128,128]{1,0:T(8,128)S(1)}, f32[128,128]{1,0:T(8,128)S(1)}, u32[]{:S(2)}, u32[]{:S(2)}) collective-permute-start(f32[128,128]{1,0:T(8,128)S(1)} %get-tuple-element.20), channel_id=1, source_target_pairs={{8,0},{9,1},{10,2},{11,3},{12,4},{13,5},{14,6},{15,7},{16,8},{17,9... | collective-permute-start | bytes 196616 | tf_op jit(solution)/shard_map/ppermute | solution.py:194
  28.0 10.4 %collective-permute-start = (f32[128,128]{1,0:T(8,128)S(1)}, f32[128,128]{1,0:T(8,128)S(1)}, u32[]{:S(2)}, u32[]{:S(2)}) collective-permute-start(f32[128,128]{1,0:T(8,128)S(1)} %get-tuple-element.21), channel_id=1, source_target_pairs={{0,8},{1,9},{2,10},{3,11},{4,12},{5,13},{6,14},{7,15},{8,16},{9,17... | collective-permute-start | bytes 196616 | tf_op jit(solution)/shard_map/ppermute | solution.py:194
  32.1 6.2 %collective-permute-start.6 = (f32[128,128]{1,0:T(8,128)S(1)}, f32[128,128]{1,0:T(8,128)S(1)}, u32[]{:S(2)}, u32[]{:S(2)}) collective-permute-start(f32[128,128]{1,0:T(8,128)S(1)} %bitcast.30), channel_id=1, source_target_pairs={{1,0},{2,1},{3,2},{4,3},{5,4},{6,5},{7,6},{9,8},{10,9},{11,10},{12... | collective-permute-start | bytes 196616 | tf_op jit(solution)/shard_map/ppermute | solution.py:194
  81.0 71.2 %all-to-all-start.1 = ((bf16[32,64,128]{2,1,0:T(8,128)(2,1)}), bf16[32,64,128]{2,1,0:T(8,128)(2,1)S(1)}, u32[]{:S(2)}, u32[]{:S(2)}) async-start(bf16[32,64,128]{2,1,0:T(8,128)(2,1)} %bitcast.28), calls=%async_computation.1 | async-start | bytes 1048576 | tf_op jit(solution)/shard_map/all_to_all | solution.py:242
  120.7 12.4 %collective-permute-start.15 = (f32[1,128]{1,0:T(1,128)S(1)}, f32[1,128]{1,0:T(1,128)S(1)}, u32[]{:S(2)}, u32[]{:S(2)}) collective-permute-start(f32[1,128]{1,0:T(1,128)S(1)} %get-tuple-element.22), channel_id=1, source_target_pairs={{9,0},{10,1},{11,2},{12,3},{13,4},{14,5},{15,6},{17,8},{18,9},{19,... | collective-permute-start | bytes 1544 | tf_op jit(solution)/shard_map/ppermute | solution.py:194
  122.0 12.4 %collective-permute-start.14 = (f32[1,128]{1,0:T(1,128)S(1)}, f32[1,128]{1,0:T(1,128)S(1)}, u32[]{:S(2)}, u32[]{:S(2)}) collective-permute-start(f32[1,128]{1,0:T(1,128)S(1)} %get-tuple-element.23), channel_id=1, source_target_pairs={{8,1},{9,2},{10,3},{11,4},{12,5},{13,6},{14,7},{16,9},{17,10},{18,... | collective-permute-start | bytes 1544 | tf_op jit(solution)/shard_map/ppermute | solution.py:194
  122.7 25.6 %collective-permute-start.9 = (f32[128,128]{1,0:T(8,128)S(1)}, f32[128,128]{1,0:T(8,128)S(1)}, u32[]{:S(2)}, u32[]{:S(2)}) collective-permute-start(f32[128,128]{1,0:T(8,128)S(1)} %slice.51), channel_id=1, source_target_pairs={{8,0},{9,1},{10,2},{11,3},{12,4},{13,5},{14,6},{15,7},{16,8},{17,9... | collective-permute-start | bytes 196616 | tf_op jit(solution)/shard_map/ppermute | solution.py:194
  124.0 24.3 %collective-permute-start.8 = (f32[128,128]{1,0:T(8,128)S(1)}, f32[128,128]{1,0:T(8,128)S(1)}, u32[]{:S(2)}, u32[]{:S(2)}) collective-permute-start(f32[128,128]{1,0:T(8,128)S(1)} %slice.50), channel_id=1, source_target_pairs={{0,8},{1,9},{2,10},{3,11},{4,12},{5,13},{6,14},{7,15},{8,16},{9,17... | collective-permute-start | bytes 196616 | tf_op jit(solution)/shard_map/ppermute | solution.py:194
  129.6 18.6 %collective-permute-start.10 = (f32[128,128]{1,0:T(8,128)S(1)}, f32[128,128]{1,0:T(8,128)S(1)}, u32[]{:S(2)}, u32[]{:S(2)}) collective-permute-start(f32[128,128]{1,0:T(8,128)S(1)} %get-tuple-element.9), channel_id=1, source_target_pairs={{0,1},{1,2},{2,3},{3,4},{4,5},{5,6},{6,7},{8,9},{9,10},{10,11},{11... | collective-permute-start | bytes 196616 | tf_op jit(solution)/shard_map/ppermute | solution.py:194
  133.0 15.3 %copy-start.15 = (f32[1,128]{1,0:T(1,128)}, f32[1,128]{1,0:T(1,128)S(1)}, u32[]{:S(2)}) copy-start(f32[1,128]{1,0:T(1,128)S(1)} %collective-permute-done.15.se_ref) | copy-start | bytes 1540
  133.0 15.3 %collective-permute-start.11 = (f32[128,128]{1,0:T(8,128)S(1)}, f32[128,128]{1,0:T(8,128)S(1)}, u32[]{:S(2)}, u32[]{:S(2)}) collective-permute-start(f32[128,128]{1,0:T(8,128)S(1)} %get-tuple-element.10), channel_id=1, source_target_pairs={{1,0},{2,1},{3,2},{4,3},{5,4},{6,5},{7,6},{9,8},{10,9},{11,10},{12... | collective-permute-start | bytes 196616 | tf_op jit(solution)/shard_map/ppermute | solution.py:194
  134.4 0.7 collective-permute-start.13
  135.1 13.2 %collective-permute-start.12 = (f32[1,128]{1,0:T(1,128)S(1)}, f32[1,128]{1,0:T(1,128)S(1)}, u32[]{:S(2)}, u32[]{:S(2)}) collective-permute-start(f32[1,128]{1,0:T(1,128)S(1)} %get-tuple-element.25), channel_id=1, source_target_pairs={{0,9},{1,10},{2,11},{3,12},{4,13},{5,14},{6,15},{8,17},{9,18},{10,... | collective-permute-start | bytes 1544 | tf_op jit(solution)/shard_map/ppermute | solution.py:194
  (13 other events, 40.4 us)

commit v2 on v1

v2 whole, which is shorter than its diff:
```python
import functools
import math
import jax
import jax.numpy as jnp
from jax import lax
from jax.experimental import pallas as pl
from jax.experimental.pallas import tpu as pltpu
from jax.sharding import PartitionSpec as P

CAP = 64
SUB = 128
ODD = 17
EDGE = 8
F32 = jnp.float32
BF16 = jnp.bfloat16
UNROLL = 8
WAYS = ((1, 0), (-1, 0), (0, 1), (0, -1), (1, 1), (1, -1), (-1, 1), (-1, -1))


def split(x):
    hi = x.astype(BF16)
    return hi, (x - hi.astype(F32)).astype(BF16)


def column(row):
    return jnp.broadcast_to(row, (128, SUB)).T


def combined(corr_ref, jac_ref, k):
    return jnp.dot(corr_ref[k], jac_ref[...], precision=lax.Precision.HIGHEST, preferred_element_type=F32)


def place(corner, cols, pitch):
    if cols & (cols - 1) == 0:
        line = lax.shift_right_logical(corner, cols.bit_length() - 1)
    else:
        line = lax.div(corner, cols)
    return corner + line * (pitch - cols) + (EDGE - 1)


def forward_kernel(pitch, chunk_slots, col_ref, frac_ref, corr_ref, jac_ref, north_ref, south_ref, west_ref, east_ref,
                   control_ref, out_ref, pad, patches, p_both, g_both, sem):
    rows, cols, _ = control_ref.shape
    fetch = pltpu.make_async_copy(control_ref, pad.at[pl.ds(1, rows), pl.ds(EDGE, cols), :], sem)
    fetch.start()
    for k in range(9):
        hi, lo = split(combined(corr_ref, jac_ref, k))
        g_both[k * 128:(k + 1) * 128, 0:128] = hi
        g_both[k * 128:(k + 1) * 128, 128:256] = lo
    flat = pad.reshape((rows + 2) * pitch, 128)
    pad[0, EDGE:EDGE + cols, :] = north_ref[...]
    pad[rows + 1, EDGE:EDGE + cols, :] = south_ref[...]
    flat[pl.ds(EDGE - 1, rows + 2, stride=pitch), :] = west_ref[EDGE - 1:EDGE + rows + 1, :]
    flat[pl.ds(EDGE + cols, rows + 2, stride=pitch), :] = east_ref[EDGE - 1:EDGE + rows + 1, :]
    fetch.wait()

    def chunk(n, carry):
        first = n * chunk_slots

        def pick(t, c):
            for v in range(UNROLL):
                s = t * UNROLL + v
                base = place(col_ref[0, first + s], cols, pitch)
                lines = [flat[pl.ds(base + r * pitch, 4), :] for r in range(4)]
                for r in range(4):
                    patches[pl.ds(s * ODD + r * 4, 4), :] = lines[r]
            return c

        lax.fori_loop(0, chunk_slots // UNROLL, pick, 0)

        def mix(m, c):
            at = pl.ds(pl.multiple_of(first + m * SUB, SUB), SUB)
            hi_at = pl.ds(pl.multiple_of(m * SUB, SUB), SUB)
            lo_at = pl.ds(pl.multiple_of(chunk_slots + m * SUB, SUB), SUB)
            f = column(frac_ref[0, 0:1, at])
            g = column(frac_ref[0, 1:2, at])
            origin = m * (SUB * ODD)
            for a in range(3):
                lat = []
                for q in range(4):
                    low = patches[pl.ds(origin + a * 4 + q, SUB, stride=ODD), :]
                    high = patches[pl.ds(origin + a * 4 + 4 + q, SUB, stride=ODD), :]
                    lat.append((1.0 - f) * low + f * high)
                for b in range(3):
                    hi, lo = split((1.0 - g) * lat[b] + g * lat[b + 1])
                    k = 3 * a + b
                    p_both[hi_at, k * 128:(k + 1) * 128] = hi
                    p_both[lo_at, k * 128:(k + 1) * 128] = lo
            return c

        lax.fori_loop(0, chunk_slots // SUB, mix, 0)
        both = jnp.dot(p_both[...], g_both[...], preferred_element_type=F32)
        hi, lo = both[0:chunk_slots], both[chunk_slots:]
        out_ref[pl.ds(pl.multiple_of(first, chunk_slots), chunk_slots), :] = (
            hi[:, 0:128] + (hi[:, 128:256] + lo[:, 0:128] + lo[:, 128:256]))
        return carry

    lax.fori_loop(0, col_ref.shape[1] // chunk_slots, chunk, 0)


def adjoint_kernel(pitch, chunk_slots, col_ref, frac_ref, corr_ref, jac_ref, weighted_ref, control_ref,
                   grad_ref, north_ref, south_ref, west_ref, east_ref, pad, patches, q_ref, gt_hi, gt_lo, sem):
    rows, cols, _ = control_ref.shape
    inner = pad.at[pl.ds(1, rows), pl.ds(EDGE, cols), :]
    fetch = pltpu.make_async_copy(control_ref, inner, sem)
    fetch.start()
    for k in range(9):
        hi, lo = split(combined(corr_ref, jac_ref, k).T)
        for half in range(2):
            gt_hi[half * 128:(half + 1) * 128, k * 128:(k + 1) * 128] = hi
            gt_lo[half * 128:(half + 1) * 128, k * 128:(k + 1) * 128] = lo
    for i in (0, rows + 1):
        pad[i] = jnp.zeros((pitch, 128), F32)

    def clear(i, c):
        pad[pl.ds(i, 1), 0:EDGE, :] = jnp.zeros((1, EDGE, 128), F32)
        pad[pl.ds(i, 1), EDGE + cols:pitch, :] = jnp.zeros((1, pitch - cols - EDGE, 128), F32)
        return c

    lax.fori_loop(1, rows + 1, clear, 0)
    fetch.wait()
    flat = pad.reshape((rows + 2) * pitch, 128)

    def chunk(n, carry):
        first = n * chunk_slots
        w_hi, w_lo = split(weighted_ref[pl.ds(pl.multiple_of(first, chunk_slots), chunk_slots), :])
        w = jnp.concatenate([w_hi, w_lo], axis=1)
        q_ref[...] = (jnp.dot(w, gt_hi[...], preferred_element_type=F32)
                      + jnp.dot(w, gt_lo[...], preferred_element_type=F32))

        def mix(m, carry):
            at = pl.ds(pl.multiple_of(first + m * SUB, SUB), SUB)
            here = pl.ds(pl.multiple_of(m * SUB, SUB), SUB)
            f = column(frac_ref[0, 0:1, at])
            g = column(frac_ref[0, 1:2, at])
            origin = m * (SUB * ODD)
            for c in range(4):
                line = []
                for a in range(3):
                    part = None
                    if c < 3:
                        part = (1.0 - g) * q_ref[here, (3 * a + c) * 128:(3 * a + c + 1) * 128]
                    if c > 0:
                        other = g * q_ref[here, (3 * a + c - 1) * 128:(3 * a + c) * 128]
                        part = other if part is None else part + other
                    line.append(part)
                for r in range(4):
                    part = None
                    if r < 3:
                        part = (1.0 - f) * line[r]
                    if r > 0:
                        other = f * line[r - 1]
                        part = other if part is None else part + other
                    patches[pl.ds(origin + r * 4 + c, SUB, stride=ODD), :] = part
            return carry

        lax.fori_loop(0, chunk_slots // SUB, mix, 0)

        def spread(t, c):
            for v in range(UNROLL):
                s = t * UNROLL + v
                base = place(col_ref[0, first + s], cols, pitch)
                lines = [flat[pl.ds(base + r * pitch, 4), :] + patches[pl.ds(s * ODD + r * 4, 4), :] for r in range(4)]
                for r in range(4):
                    flat[pl.ds(base + r * pitch, 4), :] = lines[r]
            return c

        lax.fori_loop(0, chunk_slots // UNROLL, spread, 0)
        return carry

    lax.fori_loop(0, col_ref.shape[1] // chunk_slots, chunk, 0)
    send = pltpu.make_async_copy(inner, grad_ref, sem)
    send.start()
    north_ref[...] = pad[0]
    south_ref[...] = pad[rows + 1]
    west_ref[...] = flat[pl.ds(pitch + EDGE - 1, rows, stride=pitch), :]
    east_ref[...] = flat[pl.ds(pitch + EDGE + cols, rows, stride=pitch), :]
    send.wait()


def neighbour(way):
    p = lax.axis_index("lat") + way[0]
    q = lax.axis_index("lon") + way[1]
    inside = (p >= 0) & (p < lax.axis_size("lat")) & (q >= 0) & (q < lax.axis_size("lon"))
    return (p, q), inside


def greet():
    barrier = pltpu.get_barrier_semaphore()
    for way in WAYS:
        device, inside = neighbour(way)

        @pl.when(inside)
        def _(device=device):
            pl.semaphore_signal(barrier, inc=1, device_id=device, device_id_type=pl.DeviceIdType.MESH)

    p, q = lax.axis_index("lat"), lax.axis_index("lon")
    near_lat = jnp.minimum(p + 1, lax.axis_size("lat") - 1) - jnp.maximum(p - 1, 0) + 1
    near_lon = jnp.minimum(q + 1, lax.axis_size("lon") - 1) - jnp.maximum(q - 1, 0) + 1
    pl.semaphore_wait(barrier, near_lat * near_lon - 1)


def exchange(moves, send_sems, recv_sems):
    def copy(i):
        way = WAYS[i]
        device, inside = neighbour(way)
        source, target = moves[way]
        return pltpu.make_async_remote_copy(
            src_ref=source, dst_ref=target, send_sem=send_sems.at[i], recv_sem=recv_sems.at[i],
            device_id=device, device_id_type=pl.DeviceIdType.MESH), inside

    for i in range(len(WAYS)):
        _, inside = neighbour(WAYS[i])

        @pl.when(inside)
        def _(i=i):
            copy(i)[0].start()

    for i in range(len(WAYS)):
        _, behind = neighbour((-WAYS[i][0], -WAYS[i][1]))

        @pl.when(jnp.logical_not(behind))
        def _(i=i):
            target = moves[WAYS[i]][1]
            target[...] = jnp.zeros(target.shape, F32)

    for i in range(len(WAYS)):
        _, inside = neighbour(WAYS[i])
        _, behind = neighbour((-WAYS[i][0], -WAYS[i][1]))

        @pl.when(inside)
        def _(i=i):
            copy(i)[0].wait_send()

        @pl.when(behind)
        def _(i=i):
            copy(i)[0].wait_recv()


def halo_kernel(control_ref, north_ref, south_ref, west_ref, east_ref, tiles, ends, sides, send_sems, recv_sems, sems):
    rows, cols, _ = control_ref.shape
    loads = [
        pltpu.make_async_copy(control_ref.at[:, pl.ds(0, 8), :], tiles.at[0], sems.at[0]),
        pltpu.make_async_copy(control_ref.at[:, pl.ds(cols - 8, 8), :], tiles.at[1], sems.at[1]),
        pltpu.make_async_copy(control_ref.at[0], ends.at[0], sems.at[2]),
        pltpu.make_async_copy(control_ref.at[rows - 1], ends.at[1], sems.at[3]),
    ]
    for load in loads:
        load.start()
    greet()
    for load in loads:
        load.wait()
    sides[0] = tiles[0, :, 0, :]
    sides[1] = tiles[1, :, 7, :]
    low, high = pl.ds(0, EDGE), pl.ds(rows + EDGE, EDGE)
    first, last = pl.ds(0, EDGE), pl.ds(rows - EDGE, EDGE)
    exchange({
        (1, 0): (ends.at[1], north_ref),
        (-1, 0): (ends.at[0], south_ref),
        (0, 1): (sides.at[1], west_ref.at[pl.ds(EDGE, rows), :]),
        (0, -1): (sides.at[0], east_ref.at[pl.ds(EDGE, rows), :]),
        (1, 1): (sides.at[1, last, :], west_ref.at[low, :]),
        (1, -1): (sides.at[0, last, :], east_ref.at[low, :]),
        (-1, 1): (sides.at[1, first, :], west_ref.at[high, :]),
        (-1, -1): (sides.at[0, first, :], east_ref.at[high, :]),
    }, send_sems, recv_sems)


def edges_kernel(out_n, out_s, out_w, out_e, got_n, got_s, got_w, got_e, nw, ne, sw, se, send_sems, recv_sems):
    cols = out_n.shape[0] - 2 * EDGE
    middle, low, high = pl.ds(EDGE, cols), pl.ds(0, EDGE), pl.ds(cols + EDGE, EDGE)
    greet()
    exchange({
        (1, 0): (out_s.at[middle, :], got_n),
        (-1, 0): (out_n.at[middle, :], got_s),
        (0, 1): (out_e, got_w),
        (0, -1): (out_w, got_e),
        (1, 1): (out_s.at[high, :], nw),
        (1, -1): (out_s.at[low, :], ne),
        (-1, 1): (out_n.at[high, :], sw),
        (-1, -1): (out_n.at[low, :], se),
    }, send_sems, recv_sems)


def finish_kernel(north_ref, south_ref, west_ref, east_ref, nw_ref, ne_ref, sw_ref, se_ref, grad_in,
                  grad_ref, line_n, line_s, tile_w, tile_e, sems):
    rows, cols, _ = grad_in.shape
    inner = pl.ds(1, rows - 2)
    ends = ((grad_ref.at[0], line_n), (grad_ref.at[rows - 1], line_s),
            (grad_ref.at[inner, pl.ds(0, 8), :], tile_w), (grad_ref.at[inner, pl.ds(cols - 8, 8), :], tile_e))
    loads = [pltpu.make_async_copy(far, near, sems.at[i]) for i, (far, near) in enumerate(ends)]
    for copy in loads:
        copy.start()
    for copy in loads:
        copy.wait()
    line_n[...] += north_ref[...]
    line_s[...] += south_ref[...]
    line_n[0:1, :] += west_ref[0:1, :] + nw_ref[0:1, :]
    line_n[cols - 1:cols, :] += east_ref[0:1, :] + ne_ref[7:8, :]
    line_s[0:1, :] += west_ref[rows - 1:rows, :] + sw_ref[0:1, :]
    line_s[cols - 1:cols, :] += east_ref[rows - 1:rows, :] + se_ref[7:8, :]

    flat_w = tile_w.reshape((rows - 2) * 8, 128)
    flat_e = tile_e.reshape((rows - 2) * 8, 128)
    flat_w[pl.ds(0, rows - 2, stride=8), :] += west_ref[1:rows - 1, :]
    flat_e[pl.ds(7, rows - 2, stride=8), :] += east_ref[1:rows - 1, :]
    stores = [pltpu.make_async_copy(near, far, sems.at[i]) for i, (far, near) in enumerate(ends)]
    for copy in stores:
        copy.start()
    for copy in stores:
        copy.wait()


def body(control, corr_blocks, jacobian, obs_values, obs_count, obs_col, obs_frac, obs_rinv):
    n_devices = lax.axis_size("lat") * lax.axis_size("lon")
    rows, cols, levels = control.shape
    channels = jacobian.shape[1]
    slots = obs_col.shape[1]
    pitch = cols + 2 * EDGE
    vmem = pl.BlockSpec(memory_space=pltpu.VMEM)
    smem = pl.BlockSpec(memory_space=pltpu.SMEM)
    hbm = pl.BlockSpec(memory_space=pl.ANY)

    incoming = lax.all_to_all(obs_values.reshape(n_devices, CAP, channels), ("lat", "lon"),
                              split_axis=0, concat_axis=0, tiled=True)
    def struct(count):
        return jax.ShapeDtypeStruct((count, levels), F32)

    north, south, west, east = pl.pallas_call(
        halo_kernel,
        out_shape=[struct(cols), struct(cols), struct(rows + 2 * EDGE), struct(rows + 2 * EDGE)],
        in_specs=[hbm],
        out_specs=[vmem] * 4,
        scratch_shapes=[
            pltpu.VMEM((2, rows, 8, levels), F32),
            pltpu.VMEM((2, cols, levels), F32),
            pltpu.VMEM((2, rows, levels), F32),
            pltpu.SemaphoreType.DMA((8,)),
            pltpu.SemaphoreType.DMA((8,)),
            pltpu.SemaphoreType.DMA((4,)),
        ],
        compiler_params=pltpu.CompilerParams(collective_id=0, has_side_effects=True, vmem_limit_bytes=56 * 2**20),
        name="halo",
    )(control)

    chunk_slots = math.gcd(slots, 512)
    limit = pltpu.CompilerParams(vmem_limit_bytes=56 * 2**20)
    evolved = pl.pallas_call(
        functools.partial(forward_kernel, pitch, chunk_slots),
        out_shape=jax.ShapeDtypeStruct((slots, channels), F32),
        in_specs=[smem] + [vmem] * 7 + [hbm],
        out_specs=vmem,
        scratch_shapes=[
            pltpu.VMEM((rows + 2, pitch, levels), F32),
            pltpu.VMEM((ODD * chunk_slots, levels), F32),
            pltpu.VMEM((2 * chunk_slots, 9 * levels), BF16),
            pltpu.VMEM((9 * levels, 2 * channels), BF16),
            pltpu.SemaphoreType.DMA,
        ],
        compiler_params=limit,
        cost_estimate=pl.CostEstimate(flops=2 * slots * 1152 * 512, bytes_accessed=40 * 2**20, transcendentals=0),
        name="forward",
    )(obs_col, obs_frac, corr_blocks, jacobian, north, south, west, east, control)

    departure = evolved - incoming.reshape(slots, channels).astype(F32)
    live = (jnp.arange(CAP, dtype=jnp.int32)[None, :] < obs_count[0][:, None]).reshape(slots, 1)
    weighted = jnp.where(live, obs_rinv[0][:, None] * departure, jnp.zeros_like(departure))
    returned = lax.all_to_all(weighted.astype(BF16).reshape(n_devices, CAP, channels), ("lat", "lon"),
                              split_axis=0, concat_axis=0, tiled=True)

    gradient, out_n, out_s, out_w, out_e = pl.pallas_call(
        functools.partial(adjoint_kernel, pitch, chunk_slots),
        out_shape=[
            jax.ShapeDtypeStruct(control.shape, F32),
            jax.ShapeDtypeStruct((pitch, levels), F32),
            jax.ShapeDtypeStruct((pitch, levels), F32),
            jax.ShapeDtypeStruct((rows, levels), F32),
            jax.ShapeDtypeStruct((rows, levels), F32),
        ],
        in_specs=[smem] + [vmem] * 4 + [hbm],
        out_specs=[hbm] + [vmem] * 4,
        scratch_shapes=[
            pltpu.VMEM((rows + 2, pitch, levels), F32),
            pltpu.VMEM((ODD * chunk_slots, levels), F32),
            pltpu.VMEM((chunk_slots, 9 * levels), F32),
            pltpu.VMEM((2 * channels, 9 * levels), BF16),
            pltpu.VMEM((2 * channels, 9 * levels), BF16),
            pltpu.SemaphoreType.DMA,
        ],
        compiler_params=limit,
        cost_estimate=pl.CostEstimate(flops=2 * slots * 1152 * 512, bytes_accessed=60 * 2**20, transcendentals=0),
        name="adjoint",
    )(obs_col, obs_frac, corr_blocks, jacobian, weighted, control)

    got = pl.pallas_call(
        edges_kernel,
        out_shape=[struct(cols), struct(cols), struct(rows), struct(rows)] + [struct(EDGE)] * 4,
        in_specs=[vmem] * 4,
        out_specs=[vmem] * 8,
        scratch_shapes=[pltpu.SemaphoreType.DMA((8,)), pltpu.SemaphoreType.DMA((8,))],
        compiler_params=pltpu.CompilerParams(collective_id=1, has_side_effects=True),
        name="edges",
    )(out_n, out_s, out_w, out_e)
    gradient = pl.pallas_call(
        finish_kernel,
        out_shape=jax.ShapeDtypeStruct(control.shape, F32),
        in_specs=[vmem] * 8 + [hbm],
        out_specs=hbm,
        scratch_shapes=[
            pltpu.VMEM((cols, levels), F32),
            pltpu.VMEM((cols, levels), F32),
            pltpu.VMEM((rows - 2, 8, levels), F32),
            pltpu.VMEM((rows - 2, 8, levels), F32),
            pltpu.SemaphoreType.DMA((4,)),
        ],
        input_output_aliases={8: 0},
        name="finish",
    )(*got, gradient)
    return (gradient, returned.reshape(n_devices * CAP, channels))


def solution(mesh):
    in_specs = (
        P("lat", "lon", None),
        P(),
        P(),
        P(("lat", "lon"), None),
        P(("lat", "lon"), None),
        P(("lat", "lon"), None),
        P(("lat", "lon"), None, None),
        P(("lat", "lon"), None),
    )
    out_specs = (P("lat", "lon", None), P(("lat", "lon"), None))
    return jax.shard_map(body, mesh=mesh, in_specs=in_specs, out_specs=out_specs, check_vma=False)
```

time: 155 us -> 90.1 us (0.58)
  starting transfers between devices: 60.3 us -> 16.8 us
  local copies, waits for them, and re-layouts: 14.6 us -> 0.89 us
  waiting for transfers between devices: 6.19 us -> 0.01 us
    ppermute x16 -> x0, starting transfers between devices: 47.7 us -> none  [shift(): return lax.ppermute(x, ('lat', 'lon'), pairs)]
    unnamed x39 -> x3, local copies, waits for them, and re-layouts: 11.5 us -> 0.8 us
    ppermute x16 -> x0, waiting for transfers between devices: 6.19 us -> none  [shift(): return lax.ppermute(x, ('lat', 'lon'), pairs)]
    all_to_all x1, starting transfers between devices: 5.28 us -> 9.51 us  [body(): lax.all_to_all(weighted.astype(BF16).reshape(n_devices, CAP, channels), (...]
    squeeze x2 -> x0, local copies, waits for them, and re-layouts: 1.63 us -> none  [the longest x1 0.88 us: body(): south = shift(control[0], -1, 0)]
    pallas_call x2 -> x4, Pallas kernels: 65.4 us -> 64.2 us  [the longest x1 25.5 us: body(): pl.pallas_call(functools.partial(adjoint_kernel, pitch, chunk_slots), out...]
  transfers between devices with their start and end apart: 18 -> 2, of which waited for: 2 -> 0; matrix products, arithmetic and copies ran while one was open for 2% -> 1% of each run, Pallas kernels for 45% -> 76%
where the time goes in v2:
time: 90.1 us; the launch traced here: 89.2 us
  Pallas kernels  67.5 us (75%)
  starting transfers between devices  16.8 us (19%)
  other arithmetic  3.35 us (4%)
    pallas_call x1, Pallas kernels, body(): pl.pallas_call(functools.partial(adjoint_kernel, pitch, chunk_slots), out...  25.5 us
    pallas_call x1, Pallas kernels, body(): pl.pallas_call(functools.partial(forward_kernel, pitch, chunk_slots), out...  20.7 us
    pallas_call x1, Pallas kernels, body(): pl.pallas_call(halo_kernel, out_shape=[struct(cols), struct(cols), struct...  9.76 us
    all_to_all x1, starting transfers between devices, body(): lax.all_to_all(weighted.astype(BF16).reshape(n_devices, CAP, channels), (...  9.51 us
    pallas_call x1, Pallas kernels, body(): pl.pallas_call(edges_kernel, out_shape=[struct(cols), struct(cols), struc...  8.13 us
    all_to_all x1, starting transfers between devices, body(): lax.all_to_all(obs_values.reshape(n_devices, CAP, channels), ('lat', 'lon...  7.3 us
    pallas_call x1, Pallas kernels, body(): pl.pallas_call(finish_kernel, out_shape=jax.ShapeDtypeStruct(control.shap...  3.28 us
    convert_element_type x1, other arithmetic, body(): weighted.astype(BF16).reshape(n_devices, CAP, channels)  2.62 us
  transfers between devices with their start and end apart: 2, of which 0 were waited for; matrix products, arithmetic and copies ran while one was open for 1% of the time, Pallas kernels for 76%

profile of v2, /device:TPU:0, one launch (start us, length us, event | category | flops | bytes accessed | tf_op | source)
XLA Modules:
  0.0 89.2 jit_solution(8205762192154922393)
XLA Ops:
  0.6 7.3 %all-to-all-start = ((bf16[32,64,128]{2,1,0:T(8,128)(2,1)}), bf16[32,64,128]{2,1,0:T(8,128)(2,1)S(1)}, u32[]{:S(2)}, u32[]{:S(2)}) async-start(bf16[32,64,128]{2,1,0:T(8,128)(2,1)} %bitcast.10), calls=%async_computation | async-start | bytes 1048576 | tf_op jit(solution)/shard_map/all_to_all | solution.py:324
  7.9 0.7 iota_compare_fusion
  8.7 0.1 lt.26
  8.8 0.0 copy-start
  8.8 9.8 %halo.1 = (f32[128,128]{1,0:T(8,128)}, f32[128,128]{1,0:T(8,128)}, f32[144,128]{1,0:T(8,128)}, f32[144,128]{1,0:T(8,128)}) custom-call(f32[128,128,128]{2,1,0:T(8,128)} %control_ref.5), custom_call_target="tpu_custom_call" | custom-call | tf_op jit(solution)/shard_map/halo/pallas_call | solution.py:329
  18.5 20.7 %forward.1 = f32[2048,128]{1,0:T(8,128)} custom-call(s32[1,2048]{1,0:T(1,128)} %col_ref.3, f32[1,2,2048]{2,1,0:T(2,128)} %frac_ref.3, f32[9,128,128]{2,1,0:T(8,128)} %corr_ref.3, f32[128,128]{1,0:T(8,128)} %jac_ref.3, f32[128,128]{1,0:T(8,128)} %get-tuple-element.19.north_ref, f32[128,128]{1,0:T(8,128)} %get-tuple-element.20.south_ref, ...), custom_call_target="tpu_custom_call" | custom-call | flops 2415919104 | bytes 41943040 | tf_op jit(solution)/shard_map/forward/pallas_call | solution.py:348
  39.3 0.0 all-to-all-done
  39.3 0.0 copy-done
  39.3 2.6 %fusion.2 = (bf16[2048,128]{1,0:T(8,128)(2,1)}, f32[2048,128]{1,0:T(8,128)}) fusion(f32[2048,128]{1,0:T(8,128)} %forward.1, bf16[32,64,128]{2,1,0:T(8,128)(2,1)S(1)} %all-to-all-done, f32[2048]{0:T(1024)S(1)} %bitcast.11, pred[2048]{0:T(1024)(128)(4,1)S(1)} %lt.26), kind=kLoop, calls=%fused_computation.4 | loop fusion | flops 1310720 | bytes 3155968 | tf_op jit(solution)/shard_map/convert_element_type | solution.py:368
  41.9 9.5 %all-to-all-start.1 = ((bf16[32,64,128]{2,1,0:T(8,128)(2,1)}), bf16[32,64,128]{2,1,0:T(8,128)(2,1)S(1)}, u32[]{:S(2)}, u32[]{:S(2)}) async-start(bf16[32,64,128]{2,1,0:T(8,128)(2,1)} %bitcast.4), calls=%async_computation.1 | async-start | bytes 1048576 | tf_op jit(solution)/shard_map/all_to_all | solution.py:368
  51.4 25.5 %adjoint.1 = (f32[128,128,128]{2,1,0:T(8,128)}, f32[144,128]{1,0:T(8,128)}, f32[144,128]{1,0:T(8,128)}, f32[128,128]{1,0:T(8,128)}, f32[128,128]{1,0:T(8,128)}) custom-call(s32[1,2048]{1,0:T(1,128)} %col_ref.3, f32[1,2,2048]{2,1,0:T(2,128)} %frac_ref.3, f32[9,128,128]{2,1,0:T(8,128)} %corr_ref.3, f32[128,128]{1,0:T(8,128)} %jac_ref.3, ...), custom_call_target="tpu_custom_call" | custom-call | flops 2415919104 | bytes 62914560 | tf_op jit(solution)/shard_map/adjoint/pallas_call | solution.py:371
  77.0 8.1 %edges.1 = (f32[128,128]{1,0:T(8,128)}, f32[128,128]{1,0:T(8,128)}, f32[128,128]{1,0:T(8,128)}, f32[128,128]{1,0:T(8,128)}, f32[8,128]{1,0:T(8,128)}, /*index=5*...) custom-call(f32[144,128]{1,0:T(8,128)} %get-tuple-element.23.out_n, f32[144,128]{1,0:T(8,128)} %get-tuple-element.24.out_s, ...), custom_call_target="tpu_custom_call" | custom-call | tf_op jit(solution)/shard_map/edges/pallas_call | solution.py:395
  85.1 3.3 %finish.1 = f32[128,128,128]{2,1,0:T(8,128)} custom-call(f32[128,128]{1,0:T(8,128)} %get-tuple-element.27.north_ref, f32[128,128]{1,0:T(8,128)} %get-tuple-element.28.south_ref, f32[128,128]{1,0:T(8,128)} %get-tuple-element.29.west_ref, f32[128,128]{1,0:T(8,128)} %get-tuple-element.30.east_ref, ...), custom_call_target="tpu_custom_call", output_to_operand_aliasing={{}: (8, {})} | custom-call | tf_op jit(solution)/shard_map/finish/pallas_call | solution.py:404
  88.4 0.0 all-to-all-done.1
  88.4 0.8 copy.13
Async XLA Ops:
  0.6 38.6 %all-to-all-start = ((bf16[32,64,128]{2,1,0:T(8,128)(2,1)}), bf16[32,64,128]{2,1,0:T(8,128)(2,1)S(1)}, u32[]{:S(2)}, u32[]{:S(2)}) async-start(bf16[32,64,128]{2,1,0:T(8,128)(2,1)} %bitcast.10), calls=%async_computation | async-start | bytes 1048576 | tf_op jit(solution)/shard_map/all_to_all | solution.py:324
  8.8 30.5 %copy-start = (f32[1,2048]{1,0:T(1,128)S(1)}, f32[1,2048]{1,0:T(1,128)}, u32[]{:S(2)}) copy-start(f32[1,2048]{1,0:T(1,128)} %param.15) | copy-start | bytes 24580
  41.9 46.5 %all-to-all-start.1 = ((bf16[32,64,128]{2,1,0:T(8,128)(2,1)}), bf16[32,64,128]{2,1,0:T(8,128)(2,1)S(1)}, u32[]{:S(2)}, u32[]{:S(2)}) async-start(bf16[32,64,128]{2,1,0:T(8,128)(2,1)} %bitcast.4), calls=%async_computation.1 | async-start | bytes 1048576 | tf_op jit(solution)/shard_map/all_to_all | solution.py:368

commit v3 on v2

--- a/solution.py
+++ b/solution.py
@@ -38,15 +38,12 @@
     return corner + line * (pitch - cols) + (EDGE - 1)
 
 
-def forward_kernel(pitch, chunk_slots, col_ref, frac_ref, corr_ref, jac_ref, north_ref, south_ref, west_ref, east_ref,
-                   control_ref, out_ref, pad, patches, p_both, g_both, sem):
+def forward_kernel(pitch, chunk_slots, col_ref, count_ref, frac_ref, rinv_ref, observed_ref, g_both,
+                   north_ref, south_ref, west_ref, east_ref, control_ref, weighted_ref, rounded_ref,
+                   pad, patches, p_both, sem):
     rows, cols, _ = control_ref.shape
     fetch = pltpu.make_async_copy(control_ref, pad.at[pl.ds(1, rows), pl.ds(EDGE, cols), :], sem)
     fetch.start()
-    for k in range(9):
-        hi, lo = split(combined(corr_ref, jac_ref, k))
-        g_both[k * 128:(k + 1) * 128, 0:128] = hi
-        g_both[k * 128:(k + 1) * 128, 128:256] = lo
     flat = pad.reshape((rows + 2) * pitch, 128)
     pad[0, EDGE:EDGE + cols, :] = north_ref[...]
     pad[rows + 1, EDGE:EDGE + cols, :] = south_ref[...]
@@ -58,12 +55,13 @@
         first = n * chunk_slots
 
         def pick(t, c):
+            lines = []
             for v in range(UNROLL):
-                s = t * UNROLL + v
-                base = place(col_ref[0, first + s], cols, pitch)
-                lines = [flat[pl.ds(base + r * pitch, 4), :] for r in range(4)]
+                base = place(col_ref[0, first + t * UNROLL + v], cols, pitch)
+                lines.append([flat[pl.ds(base + r * pitch, 4), :] for r in range(4)])
+            for v in range(UNROLL):
                 for r in range(4):
-                    patches[pl.ds(s * ODD + r * 4, 4), :] = lines[r]
+                    patches[pl.ds((t * UNROLL + v) * ODD + r * 4, 4), :] = lines[v][r]
             return c
 
         lax.fori_loop(0, chunk_slots // UNROLL, pick, 0)
@@ -90,25 +88,31 @@
 
         lax.fori_loop(0, chunk_slots // SUB, mix, 0)
         both = jnp.dot(p_both[...], g_both[...], preferred_element_type=F32)
-        hi, lo = both[0:chunk_slots], both[chunk_slots:]
-        out_ref[pl.ds(pl.multiple_of(first, chunk_slots), chunk_slots), :] = (
-            hi[:, 0:128] + (hi[:, 128:256] + lo[:, 0:128] + lo[:, 128:256]))
+        for m in range(chunk_slots // SUB):
+            hi, lo = both[m * SUB:(m + 1) * SUB], both[chunk_slots + m * SUB:chunk_slots + (m + 1) * SUB]
+            evolved = hi[:, 0:128] + (hi[:, 128:256] + lo[:, 0:128] + lo[:, 128:256])
+            start = pl.multiple_of(first + m * SUB, SUB)
+            at = pl.ds(start, SUB)
+            lane = lax.broadcasted_iota(jnp.int32, (1, SUB), 1)
+            live = jnp.zeros((1, SUB), jnp.int32)
+            for part in range(SUB // CAP):
+                count = count_ref[0, n * (chunk_slots // CAP) + m * (SUB // CAP) + part]
+                live += ((lane >= part * CAP) & (lane < part * CAP + count)).astype(jnp.int32)
+            rinv = jnp.where(live > 0, rinv_ref[0:1, at], 0.0)
+            weighted = column(rinv) * (evolved - observed_ref[at, :].astype(F32))
+            weighted_ref[at, :] = weighted
+            rounded_ref[at, :] = weighted.astype(BF16)
         return carry
 
     lax.fori_loop(0, col_ref.shape[1] // chunk_slots, chunk, 0)
 
 
-def adjoint_kernel(pitch, chunk_slots, col_ref, frac_ref, corr_ref, jac_ref, weighted_ref, control_ref,
-                   grad_ref, north_ref, south_ref, west_ref, east_ref, pad, patches, q_ref, gt_hi, gt_lo, sem):
+def adjoint_kernel(pitch, chunk_slots, col_ref, frac_ref, gt_hi, gt_lo, weighted_ref, control_ref,
+                   grad_ref, north_ref, south_ref, west_ref, east_ref, pad, patches, q_ref, sem):
     rows, cols, _ = control_ref.shape
     inner = pad.at[pl.ds(1, rows), pl.ds(EDGE, cols), :]
     fetch = pltpu.make_async_copy(control_ref, inner, sem)
     fetch.start()
-    for k in range(9):
-        hi, lo = split(combined(corr_ref, jac_ref, k).T)
-        for half in range(2):
-            gt_hi[half * 128:(half + 1) * 128, k * 128:(k + 1) * 128] = hi
-            gt_lo[half * 128:(half + 1) * 128, k * 128:(k + 1) * 128] = lo
     for i in (0, rows + 1):
         pad[i] = jnp.zeros((pitch, 128), F32)
 
@@ -157,12 +161,15 @@
         lax.fori_loop(0, chunk_slots // SUB, mix, 0)
 
         def spread(t, c):
+            bases, terms = [], []
             for v in range(UNROLL):
                 s = t * UNROLL + v
-                base = place(col_ref[0, first + s], cols, pitch)
-                lines = [flat[pl.ds(base + r * pitch, 4), :] + patches[pl.ds(s * ODD + r * 4, 4), :] for r in range(4)]
+                bases.append(place(col_ref[0, first + s], cols, pitch))
+                terms.append([patches[pl.ds(s * ODD + r * 4, 4), :] for r in range(4)])
+            for v in range(UNROLL):
+                lines = [flat[pl.ds(bases[v] + r * pitch, 4), :] + terms[v][r] for r in range(4)]
                 for r in range(4):
-                    flat[pl.ds(base + r * pitch, 4), :] = lines[r]
+                    flat[pl.ds(bases[v] + r * pitch, 4), :] = lines[r]
             return c
 
         lax.fori_loop(0, chunk_slots // UNROLL, spread, 0)
@@ -185,19 +192,63 @@
     return (p, q), inside
 
 
+def everyone():
+    n_lon = lax.axis_size("lon")
+    count = lax.axis_size("lat") * n_lon
+    return lax.axis_index("lat") * n_lon + lax.axis_index("lon"), count, n_lon
+
+
 def greet():
+    me, count, n_lon = everyone()
     barrier = pltpu.get_barrier_semaphore()
-    for way in WAYS:
-        device, inside = neighbour(way)
-
-        @pl.when(inside)
-        def _(device=device):
-            pl.semaphore_signal(barrier, inc=1, device_id=device, device_id_type=pl.DeviceIdType.MESH)
-
-    p, q = lax.axis_index("lat"), lax.axis_index("lon")
-    near_lat = jnp.minimum(p + 1, lax.axis_size("lat") - 1) - jnp.maximum(p - 1, 0) + 1
-    near_lon = jnp.minimum(q + 1, lax.axis_size("lon") - 1) - jnp.maximum(q - 1, 0) + 1
-    pl.semaphore_wait(barrier, near_lat * near_lon - 1)
+
+    def signal(k, c):
+        peer = lax.rem(me + k, count)
+        pl.semaphore_signal(barrier, inc=1, device_id=(lax.div(peer, n_lon), lax.rem(peer, n_lon)),
+                            device_id_type=pl.DeviceIdType.MESH)
+        return c
+
+    lax.fori_loop(1, count, signal, 0)
+    pl.semaphore_wait(barrier, count - 1)
+
+
+def swap_blocks(source, target, send_sems, recv_sems, own_sem):
+    me, count, n_lon = everyone()
+
+    def block(ref, d):
+        return ref.at[pl.ds(pl.multiple_of(d * CAP, CAP), CAP), :]
+
+    def copy(k):
+        peer = lax.rem(me + k, count)
+        return pltpu.make_async_remote_copy(
+            src_ref=block(source, peer), dst_ref=block(target, me), send_sem=send_sems.at[k], recv_sem=recv_sems.at[k],
+            device_id=(lax.div(peer, n_lon), lax.rem(peer, n_lon)), device_id_type=pl.DeviceIdType.MESH)
+
+    own = pltpu.make_async_copy(block(source, me), block(target, me), own_sem)
+
+    def start():
+        own.start()
+
+        def one(k, c):
+            copy(k).start()
+            return c
+
+        lax.fori_loop(1, count, one, 0)
+
+    def wait():
+        def one(k, c):
+            copy(k).wait_send()
+            came = lax.rem(me - k + count, count)
+            pltpu.make_async_remote_copy(
+                src_ref=block(source, came), dst_ref=block(target, came), send_sem=send_sems.at[k],
+                recv_sem=recv_sems.at[k], device_id=(lax.div(came, n_lon), lax.rem(came, n_lon)),
+                device_id_type=pl.DeviceIdType.MESH).wait_recv()
+            return c
+
+        lax.fori_loop(1, count, one, 0)
+        own.wait()
+
+    return start, wait
 
 
 def exchange(moves, send_sems, recv_sems):
@@ -209,35 +260,41 @@
             src_ref=source, dst_ref=target, send_sem=send_sems.at[i], recv_sem=recv_sems.at[i],
             device_id=device, device_id_type=pl.DeviceIdType.MESH), inside
 
-    for i in range(len(WAYS)):
-        _, inside = neighbour(WAYS[i])
-
-        @pl.when(inside)
-        def _(i=i):
-            copy(i)[0].start()
-
-    for i in range(len(WAYS)):
-        _, behind = neighbour((-WAYS[i][0], -WAYS[i][1]))
-
-        @pl.when(jnp.logical_not(behind))
-        def _(i=i):
-            target = moves[WAYS[i]][1]
-            target[...] = jnp.zeros(target.shape, F32)
-
-    for i in range(len(WAYS)):
-        _, inside = neighbour(WAYS[i])
-        _, behind = neighbour((-WAYS[i][0], -WAYS[i][1]))
-
-        @pl.when(inside)
-        def _(i=i):
-            copy(i)[0].wait_send()
-
-        @pl.when(behind)
-        def _(i=i):
-            copy(i)[0].wait_recv()
-
-
-def halo_kernel(control_ref, north_ref, south_ref, west_ref, east_ref, tiles, ends, sides, send_sems, recv_sems, sems):
+    def start():
+        for i in range(len(WAYS)):
+            _, inside = neighbour(WAYS[i])
+
+            @pl.when(inside)
+            def _(i=i):
+                copy(i)[0].start()
+
+    def wait():
+        for i in range(len(WAYS)):
+            _, behind = neighbour((-WAYS[i][0], -WAYS[i][1]))
+
+            @pl.when(jnp.logical_not(behind))
+            def _(i=i):
+                target = moves[WAYS[i]][1]
+                target[...] = jnp.zeros(target.shape, F32)
+
+        for i in range(len(WAYS)):
+            _, inside = neighbour(WAYS[i])
+            _, behind = neighbour((-WAYS[i][0], -WAYS[i][1]))
+
+            @pl.when(inside)
+            def _(i=i):
+                copy(i)[0].wait_send()
+
+            @pl.when(behind)
+            def _(i=i):
+                copy(i)[0].wait_recv()
+
+    return start, wait
+
+
+def front_kernel(control_ref, values_ref, corr_ref, jac_ref,
+                 north_ref, south_ref, west_ref, east_ref, observed_ref, g_both, gt_hi, gt_lo,
+                 tiles, ends, sides, send_sems, recv_sems, sems, far_send, far_recv):
     rows, cols, _ = control_ref.shape
     loads = [
         pltpu.make_async_copy(control_ref.at[:, pl.ds(0, 8), :], tiles.at[0], sems.at[0]),
@@ -254,7 +311,7 @@
     sides[1] = tiles[1, :, 7, :]
     low, high = pl.ds(0, EDGE), pl.ds(rows + EDGE, EDGE)
     first, last = pl.ds(0, EDGE), pl.ds(rows - EDGE, EDGE)
-    exchange({
+    start_halo, wait_halo = exchange({
         (1, 0): (ends.at[1], north_ref),
         (-1, 0): (ends.at[0], south_ref),
         (0, 1): (sides.at[1], west_ref.at[pl.ds(EDGE, rows), :]),
@@ -264,13 +321,28 @@
         (-1, 1): (sides.at[1, first, :], west_ref.at[high, :]),
         (-1, -1): (sides.at[0, first, :], east_ref.at[high, :]),
     }, send_sems, recv_sems)
-
-
-def edges_kernel(out_n, out_s, out_w, out_e, got_n, got_s, got_w, got_e, nw, ne, sw, se, send_sems, recv_sems):
+    start_blocks, wait_blocks = swap_blocks(values_ref, observed_ref, far_send, far_recv, sems.at[4])
+    start_halo()
+    start_blocks()
+    for k in range(9):
+        g = combined(corr_ref, jac_ref, k)
+        hi, lo = split(g)
+        g_both[k * 128:(k + 1) * 128, 0:128] = hi
+        g_both[k * 128:(k + 1) * 128, 128:256] = lo
+        hi, lo = split(g.T)
+        for half in range(2):
+            gt_hi[half * 128:(half + 1) * 128, k * 128:(k + 1) * 128] = hi
+            gt_lo[half * 128:(half + 1) * 128, k * 128:(k + 1) * 128] = lo
+    wait_halo()
+    wait_blocks()
+
+
+def back_kernel(out_n, out_s, out_w, out_e, rounded_ref, got_n, got_s, got_w, got_e, nw, ne, sw, se, returned_ref,
+                send_sems, recv_sems, far_send, far_recv, own_sem):
     cols = out_n.shape[0] - 2 * EDGE
     middle, low, high = pl.ds(EDGE, cols), pl.ds(0, EDGE), pl.ds(cols + EDGE, EDGE)
     greet()
-    exchange({
+    start_edges, wait_edges = exchange({
         (1, 0): (out_s.at[middle, :], got_n),
         (-1, 0): (out_n.at[middle, :], got_s),
         (0, 1): (out_e, got_w),
@@ -280,6 +352,11 @@
         (-1, 1): (out_n.at[high, :], sw),
         (-1, -1): (out_n.at[low, :], se),
     }, send_sems, recv_sems)
+    start_blocks, wait_blocks = swap_blocks(rounded_ref, returned_ref, far_send, far_recv, own_sem)
+    start_edges()
+    start_blocks()
+    wait_edges()
+    wait_blocks()
 
 
 def finish_kernel(north_ref, south_ref, west_ref, east_ref, nw_ref, ne_ref, sw_ref, se_ref, grad_in,
@@ -321,52 +398,49 @@
     smem = pl.BlockSpec(memory_space=pltpu.SMEM)
     hbm = pl.BlockSpec(memory_space=pl.ANY)
 
-    incoming = lax.all_to_all(obs_values.reshape(n_devices, CAP, channels), ("lat", "lon"),
-                              split_axis=0, concat_axis=0, tiled=True)
     def struct(count):
         return jax.ShapeDtypeStruct((count, levels), F32)
 
-    north, south, west, east = pl.pallas_call(
-        halo_kernel,
-        out_shape=[struct(cols), struct(cols), struct(rows + 2 * EDGE), struct(rows + 2 * EDGE)],
-        in_specs=[hbm],
-        out_specs=[vmem] * 4,
+    north, south, west, east, observed, g_both, gt_hi, gt_lo = pl.pallas_call(
+        front_kernel,
+        out_shape=[struct(cols), struct(cols), struct(rows + 2 * EDGE), struct(rows + 2 * EDGE),
+                   jax.ShapeDtypeStruct((slots, channels), BF16),
+                   jax.ShapeDtypeStruct((9 * levels, 2 * channels), BF16),
+                   jax.ShapeDtypeStruct((2 * channels, 9 * levels), BF16),
+                   jax.ShapeDtypeStruct((2 * channels, 9 * levels), BF16)],
+        in_specs=[hbm, hbm, vmem, vmem],
+        out_specs=[vmem] * 8,
         scratch_shapes=[
             pltpu.VMEM((2, rows, 8, levels), F32),
             pltpu.VMEM((2, cols, levels), F32),
             pltpu.VMEM((2, rows, levels), F32),
             pltpu.SemaphoreType.DMA((8,)),
             pltpu.SemaphoreType.DMA((8,)),
-            pltpu.SemaphoreType.DMA((4,)),
+            pltpu.SemaphoreType.DMA((5,)),
+            pltpu.SemaphoreType.DMA((n_devices,)),
+            pltpu.SemaphoreType.DMA((n_devices,)),
         ],
         compiler_params=pltpu.CompilerParams(collective_id=0, has_side_effects=True, vmem_limit_bytes=56 * 2**20),
-        name="halo",
-    )(control)
+        name="front",
+    )(control, obs_values, corr_blocks, jacobian)
 
     chunk_slots = math.gcd(slots, 512)
     limit = pltpu.CompilerParams(vmem_limit_bytes=56 * 2**20)
-    evolved = pl.pallas_call(
+    weighted, rounded = pl.pallas_call(
         functools.partial(forward_kernel, pitch, chunk_slots),
-        out_shape=jax.ShapeDtypeStruct((slots, channels), F32),
-        in_specs=[smem] + [vmem] * 7 + [hbm],
-        out_specs=vmem,
+        out_shape=[jax.ShapeDtypeStruct((slots, channels), F32), jax.ShapeDtypeStruct((slots, channels), BF16)],
+        in_specs=[smem, smem] + [vmem] * 8 + [hbm],
+        out_specs=[vmem, vmem],
         scratch_shapes=[
             pltpu.VMEM((rows + 2, pitch, levels), F32),
             pltpu.VMEM((ODD * chunk_slots, levels), F32),
             pltpu.VMEM((2 * chunk_slots, 9 * levels), BF16),
-            pltpu.VMEM((9 * levels, 2 * channels), BF16),
             pltpu.SemaphoreType.DMA,
         ],
         compiler_params=limit,
         cost_estimate=pl.CostEstimate(flops=2 * slots * 1152 * 512, bytes_accessed=40 * 2**20, transcendentals=0),
         name="forward",
-    )(obs_col, obs_frac, corr_blocks, jacobian, north, south, west, east, control)
-
-    departure = evolved - incoming.reshape(slots, channels).astype(F32)
-    live = (jnp.arange(CAP, dtype=jnp.int32)[None, :] < obs_count[0][:, None]).reshape(slots, 1)
-    weighted = jnp.where(live, obs_rinv[0][:, None] * departure, jnp.zeros_like(departure))
-    returned = lax.all_to_all(weighted.astype(BF16).reshape(n_devices, CAP, channels), ("lat", "lon"),
-                              split_axis=0, concat_axis=0, tiled=True)
+    )(obs_col, obs_count, obs_frac, obs_rinv, observed, g_both, north, south, west, east, control)
 
     gradient, out_n, out_s, out_w, out_e = pl.pallas_call(
         functools.partial(adjoint_kernel, pitch, chunk_slots),
@@ -383,24 +457,29 @@
             pltpu.VMEM((rows + 2, pitch, levels), F32),
             pltpu.VMEM((ODD * chunk_slots, levels), F32),
             pltpu.VMEM((chunk_slots, 9 * levels), F32),
-            pltpu.VMEM((2 * channels, 9 * levels), BF16),
-            pltpu.VMEM((2 * channels, 9 * levels), BF16),
             pltpu.SemaphoreType.DMA,
         ],
         compiler_params=limit,
         cost_estimate=pl.CostEstimate(flops=2 * slots * 1152 * 512, bytes_accessed=60 * 2**20, transcendentals=0),
         name="adjoint",
-    )(obs_col, obs_frac, corr_blocks, jacobian, weighted, control)
-
-    got = pl.pallas_call(
-        edges_kernel,
-        out_shape=[struct(cols), struct(cols), struct(rows), struct(rows)] + [struct(EDGE)] * 4,
-        in_specs=[vmem] * 4,
-        out_specs=[vmem] * 8,
-        scratch_shapes=[pltpu.SemaphoreType.DMA((8,)), pltpu.SemaphoreType.DMA((8,))],
+    )(obs_col, obs_frac, gt_hi, gt_lo, weighted, control)
+
+    *got, returned = pl.pallas_call(
+        back_kernel,
+        out_shape=[struct(cols), struct(cols), struct(rows), struct(rows)] + [struct(EDGE)] * 4
+        + [jax.ShapeDtypeStruct((slots, channels), BF16)],
+        in_specs=[vmem] * 4 + [hbm],
+        out_specs=[vmem] * 9,
+        scratch_shapes=[
+            pltpu.SemaphoreType.DMA((8,)),
+            pltpu.SemaphoreType.DMA((8,)),
+            pltpu.SemaphoreType.DMA((n_devices,)),
+            pltpu.SemaphoreType.DMA((n_devices,)),
+            pltpu.SemaphoreType.DMA,
+        ],
         compiler_params=pltpu.CompilerParams(collective_id=1, has_side_effects=True),
-        name="edges",
-    )(out_n, out_s, out_w, out_e)
+        name="back",
+    )(out_n, out_s, out_w, out_e, rounded)
     gradient = pl.pallas_call(
         finish_kernel,
         out_shape=jax.ShapeDtypeStruct(control.shape, F32),
@@ -416,7 +495,7 @@
         input_output_aliases={8: 0},
         name="finish",
     )(*got, gradient)
-    return (gradient, returned.reshape(n_devices * CAP, channels))
+    return (gradient, returned)
 
 
 def solution(mesh):

time: 90.1 us -> 95.1 us (1.055)
  Pallas kernels: 67.5 us -> 93.2 us
  starting transfers between devices: 16.8 us -> 0 us
  other arithmetic: 3.35 us -> 0 us
    pallas_call x2, Pallas kernels: 17.9 us -> 44.1 us  [the longest x1 24.2 us: body(): pl.pallas_call(front_kernel, out_shape=[struct(cols), struct(cols), struc...]
    all_to_all x2 -> x0, starting transfers between devices: 16.8 us -> none  [the longest x1 9.51 us: body(): lax.all_to_all(weighted.astype(BF16).reshape(n_devices, CAP, channels), (...]
    convert_element_type x1 -> x0, other arithmetic: 2.62 us -> none  [body(): weighted.astype(BF16).reshape(n_devices, CAP, channels)]
  transfers between devices with their start and end apart: 2 -> 0, of which waited for: 0 -> 0; matrix products, arithmetic and copies ran while one was open for 1% -> 0% of each run, Pallas kernels for 76% -> 0%
where the time goes in v3:
time: 95.1 us; the launch traced here: 94.7 us
  Pallas kernels  93.2 us (98%)
    pallas_call x1, Pallas kernels, body(): pl.pallas_call(functools.partial(adjoint_kernel, pitch, chunk_slots), out...  24.7 us
    pallas_call x1, Pallas kernels, body(): pl.pallas_call(front_kernel, out_shape=[struct(cols), struct(cols), struc...  24.2 us
    pallas_call x1, Pallas kernels, body(): pl.pallas_call(functools.partial(forward_kernel, pitch, chunk_slots), out...  21.1 us
    pallas_call x1, Pallas kernels, body(): pl.pallas_call(back_kernel, out_shape=[struct(cols), struct(cols), struct...  19.9 us
    pallas_call x1, Pallas kernels, body(): pl.pallas_call(finish_kernel, out_shape=jax.ShapeDtypeStruct(control.shap...  3.33 us

profile of v3, /device:TPU:0, one launch (start us, length us, event | category | flops | bytes accessed | tf_op | source)
XLA Modules:
  0.0 94.7 jit_solution(9338415000050125254)
XLA Ops:
  0.6 24.2 %front.1 = (f32[128,128]{1,0:T(8,128)}, f32[128,128]{1,0:T(8,128)}, f32[144,128]{1,0:T(8,128)}, f32[144,128]{1,0:T(8,128)}, bf16[2048,128]{1,0:T(8,128)(2,1)}, /...) custom-call(f32[128,128,128]{2,1,0:T(8,128)} %control_ref.5, ...), custom_call_target="tpu_custom_call" | custom-call | tf_op jit(solution)/shard_map/front/pallas_call | solution.py:404
  24.8 21.1 %forward.1 = (f32[2048,128]{1,0:T(8,128)}, bf16[2048,128]{1,0:T(8,128)(2,1)}) custom-call(s32[1,2048]{1,0:T(1,128)} %col_ref.3, s32[1,32]{1,0:T(1,128)} %count_ref.1, f32[1,2,2048]{2,1,0:T(2,128)} %frac_ref.3, f32[1,2048]{1,0:T(1,128)} %rinv_ref.1, bf16[2048,128]{1,0:T(8,128)(2,1)} %get-tuple-element.28.observed_ref, ...), custom_call_target="tpu_custom_call" | custom-call | flops 2415919104 | bytes 41943040 | tf_op jit(solution)/shard_map/forward/pallas_call | solution.py:429
  45.9 24.7 %adjoint.1 = (f32[128,128,128]{2,1,0:T(8,128)}, f32[144,128]{1,0:T(8,128)}, f32[144,128]{1,0:T(8,128)}, f32[128,128]{1,0:T(8,128)}, f32[128,128]{1,0:T(8,128)}) custom-call(s32[1,2048]{1,0:T(1,128)} %col_ref.3, f32[1,2,2048]{2,1,0:T(2,128)} %frac_ref.3, bf16[256,1152]{1,0:T(8,128)(2,1)} %get-tuple-element.26.gt_hi, ...), custom_call_target="tpu_custom_call" | custom-call | flops 2415919104 | bytes 62914560 | tf_op jit(solution)/shard_map/adjoint/pallas_call | solution.py:445
  70.6 19.9 %back.1 = (f32[128,128]{1,0:T(8,128)}, f32[128,128]{1,0:T(8,128)}, f32[128,128]{1,0:T(8,128)}, f32[128,128]{1,0:T(8,128)}, f32[8,128]{1,0:T(8,128)}, /*index=5*/...) custom-call(f32[144,128]{1,0:T(8,128)} %get-tuple-element.35.out_n, ...), custom_call_target="tpu_custom_call" | custom-call | tf_op jit(solution)/shard_map/back/pallas_call | solution.py:467
  90.6 0.0 copy-start
  90.6 3.3 %finish.1 = f32[128,128,128]{2,1,0:T(8,128)} custom-call(f32[128,128]{1,0:T(8,128)} %get-tuple-element.40.north_ref, f32[128,128]{1,0:T(8,128)} %get-tuple-element.41.south_ref, f32[128,128]{1,0:T(8,128)} %get-tuple-element.42.west_ref, f32[128,128]{1,0:T(8,128)} %get-tuple-element.43.east_ref, ...), custom_call_target="tpu_custom_call", output_to_operand_aliasing={{}: (8, {})} | custom-call | tf_op jit(solution)/shard_map/finish/pallas_call | solution.py:483
  93.9 0.0 copy-done
  93.9 0.8 copy.13
Async XLA Ops:
  90.6 3.4 %copy-start = (bf16[2048,128]{1,0:T(8,128)(2,1)S(1)}, bf16[2048,128]{1,0:T(8,128)(2,1)}, u32[]{:S(2)}) copy-start(bf16[2048,128]{1,0:T(8,128)(2,1)} %get-tuple-element.53) | copy-start | bytes 1572868

commit v4 on v3

--- a/solution.py
+++ b/solution.py
@@ -13,7 +13,6 @@
 EDGE = 8
 F32 = jnp.float32
 BF16 = jnp.bfloat16
-UNROLL = 8
 WAYS = ((1, 0), (-1, 0), (0, 1), (0, -1), (1, 1), (1, -1), (-1, 1), (-1, -1))
 
 
@@ -40,7 +39,7 @@
 
 def forward_kernel(pitch, chunk_slots, col_ref, count_ref, frac_ref, rinv_ref, observed_ref, g_both,
                    north_ref, south_ref, west_ref, east_ref, control_ref, weighted_ref, rounded_ref,
-                   pad, patches, p_both, sem):
+                   pad, patches_a, patches_b, f_ref, g_ref, p_both, sem):
     rows, cols, _ = control_ref.shape
     fetch = pltpu.make_async_copy(control_ref, pad.at[pl.ds(1, rows), pl.ds(EDGE, cols), :], sem)
     fetch.start()
@@ -54,39 +53,43 @@
     def chunk(n, carry):
         first = n * chunk_slots
 
-        def pick(t, c):
-            lines = []
-            for v in range(UNROLL):
-                base = place(col_ref[0, first + t * UNROLL + v], cols, pitch)
-                lines.append([flat[pl.ds(base + r * pitch, 4), :] for r in range(4)])
-            for v in range(UNROLL):
+        for m in range(chunk_slots // SUB):
+            at = pl.ds(pl.multiple_of(first + m * SUB, SUB), SUB)
+            f_ref[m * SUB:(m + 1) * SUB, :] = column(frac_ref[0, 0:1, at])
+            g_ref[m * SUB:(m + 1) * SUB, :] = column(frac_ref[0, 1:2, at])
+
+        def pick(start, patches):
+            for v in range(8):
+                base = place(col_ref[0, first + start + v], cols, pitch)
                 for r in range(4):
-                    patches[pl.ds((t * UNROLL + v) * ODD + r * 4, 4), :] = lines[v][r]
+                    patches[v * ODD + r * 4:v * ODD + r * 4 + 4, :] = flat[pl.ds(base + r * pitch, 4), :]
+
+        def mix(start, patches):
+            at = pl.ds(pl.multiple_of(start, 8), 8)
+            f, g = f_ref[at, :], g_ref[at, :]
+            lines = [[patches[pl.ds(r * 4 + q, 8, stride=ODD), :] for q in range(4)] for r in range(4)]
+            mixed = []
+            for a in range(3):
+                lat = [(1.0 - f) * lines[a][q] + f * lines[a + 1][q] for q in range(4)]
+                mixed.extend((1.0 - g) * lat[b] + g * lat[b + 1] for b in range(3))
+            return mixed
+
+        def pair(t, c):
+            start = t * 16
+            upper = mix(start, patches_a)
+            pick(start + 8, patches_b)
+            lower = mix(start + 8, patches_b)
+            pick(jnp.minimum(start + 16, chunk_slots - 8), patches_a)
+            hi_at = pl.ds(pl.multiple_of(start, 16), 16)
+            lo_at = pl.ds(pl.multiple_of(chunk_slots + start, 16), 16)
+            for k in range(9):
+                hi, lo = split(jnp.concatenate([upper[k], lower[k]], axis=0))
+                p_both[hi_at, k * 128:(k + 1) * 128] = hi
+                p_both[lo_at, k * 128:(k + 1) * 128] = lo
             return c
 
-        lax.fori_loop(0, chunk_slots // UNROLL, pick, 0)
-
-        def mix(m, c):
-            at = pl.ds(pl.multiple_of(first + m * SUB, SUB), SUB)
-            hi_at = pl.ds(pl.multiple_of(m * SUB, SUB), SUB)
-            lo_at = pl.ds(pl.multiple_of(chunk_slots + m * SUB, SUB), SUB)
-            f = column(frac_ref[0, 0:1, at])
-            g = column(frac_ref[0, 1:2, at])
-            origin = m * (SUB * ODD)
-            for a in range(3):
-                lat = []
-                for q in range(4):
-                    low = patches[pl.ds(origin + a * 4 + q, SUB, stride=ODD), :]
-                    high = patches[pl.ds(origin + a * 4 + 4 + q, SUB, stride=ODD), :]
-                    lat.append((1.0 - f) * low + f * high)
-                for b in range(3):
-                    hi, lo = split((1.0 - g) * lat[b] + g * lat[b + 1])
-                    k = 3 * a + b
-                    p_both[hi_at, k * 128:(k + 1) * 128] = hi
-                    p_both[lo_at, k * 128:(k + 1) * 128] = lo
-            return c
-
-        lax.fori_loop(0, chunk_slots // SUB, mix, 0)
+        pick(0, patches_a)
+        lax.fori_loop(0, chunk_slots // 16, pair, 0, unroll=2)
         both = jnp.dot(p_both[...], g_both[...], preferred_element_type=F32)
         for m in range(chunk_slots // SUB):
             hi, lo = both[m * SUB:(m + 1) * SUB], both[chunk_slots + m * SUB:chunk_slots + (m + 1) * SUB]
@@ -108,7 +111,7 @@
 
 
 def adjoint_kernel(pitch, chunk_slots, col_ref, frac_ref, gt_hi, gt_lo, weighted_ref, control_ref,
-                   grad_ref, north_ref, south_ref, west_ref, east_ref, pad, patches, q_ref, sem):
+                   grad_ref, north_ref, south_ref, west_ref, east_ref, pad, patches_a, patches_b, f_ref, g_ref, q_ref, sem):
     rows, cols, _ = control_ref.shape
     inner = pad.at[pl.ds(1, rows), pl.ds(EDGE, cols), :]
     fetch = pltpu.make_async_copy(control_ref, inner, sem)
@@ -132,47 +135,43 @@
         q_ref[...] = (jnp.dot(w, gt_hi[...], preferred_element_type=F32)
                       + jnp.dot(w, gt_lo[...], preferred_element_type=F32))
 
-        def mix(m, carry):
+        for m in range(chunk_slots // SUB):
             at = pl.ds(pl.multiple_of(first + m * SUB, SUB), SUB)
-            here = pl.ds(pl.multiple_of(m * SUB, SUB), SUB)
-            f = column(frac_ref[0, 0:1, at])
-            g = column(frac_ref[0, 1:2, at])
-            origin = m * (SUB * ODD)
+            f_ref[m * SUB:(m + 1) * SUB, :] = column(frac_ref[0, 0:1, at])
+            g_ref[m * SUB:(m + 1) * SUB, :] = column(frac_ref[0, 1:2, at])
+
+        def mix(start, patches):
+            at = pl.ds(pl.multiple_of(start, 8), 8)
+            f, g = f_ref[at, :], g_ref[at, :]
+            rest_f, rest_g = 1.0 - f, 1.0 - g
+            q = [[q_ref[at, (3 * a + b) * 128:(3 * a + b + 1) * 128] for b in range(3)] for a in range(3)]
             for c in range(4):
                 line = []
                 for a in range(3):
-                    part = None
-                    if c < 3:
-                        part = (1.0 - g) * q_ref[here, (3 * a + c) * 128:(3 * a + c + 1) * 128]
-                    if c > 0:
-                        other = g * q_ref[here, (3 * a + c - 1) * 128:(3 * a + c) * 128]
-                        part = other if part is None else part + other
-                    line.append(part)
+                    terms = ([rest_g * q[a][c]] if c < 3 else []) + ([g * q[a][c - 1]] if c > 0 else [])
+                    line.append(sum(terms[1:], terms[0]))
                 for r in range(4):
-                    part = None
-                    if r < 3:
-                        part = (1.0 - f) * line[r]
-                    if r > 0:
-                        other = f * line[r - 1]
-                        part = other if part is None else part + other
-                    patches[pl.ds(origin + r * 4 + c, SUB, stride=ODD), :] = part
-            return carry
-
-        lax.fori_loop(0, chunk_slots // SUB, mix, 0)
-
-        def spread(t, c):
-            bases, terms = [], []
-            for v in range(UNROLL):
-                s = t * UNROLL + v
-                bases.append(place(col_ref[0, first + s], cols, pitch))
-                terms.append([patches[pl.ds(s * ODD + r * 4, 4), :] for r in range(4)])
-            for v in range(UNROLL):
-                lines = [flat[pl.ds(bases[v] + r * pitch, 4), :] + terms[v][r] for r in range(4)]
+                    terms = ([rest_f * line[r]] if r < 3 else []) + ([f * line[r - 1]] if r > 0 else [])
+                    patches[pl.ds(r * 4 + c, 8, stride=ODD), :] = sum(terms[1:], terms[0])
+
+        def spread(start, patches):
+            for v in range(8):
+                base = place(col_ref[0, first + start + v], cols, pitch)
+                lines = [flat[pl.ds(base + r * pitch, 4), :] + patches[v * ODD + r * 4:v * ODD + r * 4 + 4, :]
+                         for r in range(4)]
                 for r in range(4):
-                    flat[pl.ds(bases[v] + r * pitch, 4), :] = lines[r]
+                    flat[pl.ds(base + r * pitch, 4), :] = lines[r]
+
+        def pair(t, c):
+            start = t * 16
+            mix(start + 8, patches_b)
+            spread(start, patches_a)
+            mix(jnp.minimum(start + 16, chunk_slots - 8), patches_a)
+            spread(start + 8, patches_b)
             return c
 
-        lax.fori_loop(0, chunk_slots // UNROLL, spread, 0)
+        mix(0, patches_a)
+        lax.fori_loop(0, chunk_slots // 16, pair, 0, unroll=2)
         return carry
 
     lax.fori_loop(0, col_ref.shape[1] // chunk_slots, chunk, 0)
@@ -192,63 +191,19 @@
     return (p, q), inside
 
 
-def everyone():
-    n_lon = lax.axis_size("lon")
-    count = lax.axis_size("lat") * n_lon
-    return lax.axis_index("lat") * n_lon + lax.axis_index("lon"), count, n_lon
-
-
 def greet():
-    me, count, n_lon = everyone()
     barrier = pltpu.get_barrier_semaphore()
-
-    def signal(k, c):
-        peer = lax.rem(me + k, count)
-        pl.semaphore_signal(barrier, inc=1, device_id=(lax.div(peer, n_lon), lax.rem(peer, n_lon)),
-                            device_id_type=pl.DeviceIdType.MESH)
-        return c
-
-    lax.fori_loop(1, count, signal, 0)
-    pl.semaphore_wait(barrier, count - 1)
-
-
-def swap_blocks(source, target, send_sems, recv_sems, own_sem):
-    me, count, n_lon = everyone()
-
-    def block(ref, d):
-        return ref.at[pl.ds(pl.multiple_of(d * CAP, CAP), CAP), :]
-
-    def copy(k):
-        peer = lax.rem(me + k, count)
-        return pltpu.make_async_remote_copy(
-            src_ref=block(source, peer), dst_ref=block(target, me), send_sem=send_sems.at[k], recv_sem=recv_sems.at[k],
-            device_id=(lax.div(peer, n_lon), lax.rem(peer, n_lon)), device_id_type=pl.DeviceIdType.MESH)
-
-    own = pltpu.make_async_copy(block(source, me), block(target, me), own_sem)
-
-    def start():
-        own.start()
-
-        def one(k, c):
-            copy(k).start()
-            return c
-
-        lax.fori_loop(1, count, one, 0)
-
-    def wait():
-        def one(k, c):
-            copy(k).wait_send()
-            came = lax.rem(me - k + count, count)
-            pltpu.make_async_remote_copy(
-                src_ref=block(source, came), dst_ref=block(target, came), send_sem=send_sems.at[k],
-                recv_sem=recv_sems.at[k], device_id=(lax.div(came, n_lon), lax.rem(came, n_lon)),
-                device_id_type=pl.DeviceIdType.MESH).wait_recv()
-            return c
-
-        lax.fori_loop(1, count, one, 0)
-        own.wait()
-
-    return start, wait
+    for way in WAYS:
+        device, inside = neighbour(way)
+
+        @pl.when(inside)
+        def _(device=device):
+            pl.semaphore_signal(barrier, inc=1, device_id=device, device_id_type=pl.DeviceIdType.MESH)
+
+    p, q = lax.axis_index("lat"), lax.axis_index("lon")
+    near_lat = jnp.minimum(p + 1, lax.axis_size("lat") - 1) - jnp.maximum(p - 1, 0) + 1
+    near_lon = jnp.minimum(q + 1, lax.axis_size("lon") - 1) - jnp.maximum(q - 1, 0) + 1
+    pl.semaphore_wait(barrier, near_lat * near_lon - 1)
 
 
 def exchange(moves, send_sems, recv_sems):
@@ -292,9 +247,9 @@
     return start, wait
 
 
-def front_kernel(control_ref, values_ref, corr_ref, jac_ref,
-                 north_ref, south_ref, west_ref, east_ref, observed_ref, g_both, gt_hi, gt_lo,
-                 tiles, ends, sides, send_sems, recv_sems, sems, far_send, far_recv):
+def front_kernel(control_ref, corr_ref, jac_ref,
+                 north_ref, south_ref, west_ref, east_ref, g_both, gt_hi, gt_lo,
+                 tiles, ends, sides, send_sems, recv_sems, sems):
     rows, cols, _ = control_ref.shape
     loads = [
         pltpu.make_async_copy(control_ref.at[:, pl.ds(0, 8), :], tiles.at[0], sems.at[0]),
@@ -321,9 +276,7 @@
         (-1, 1): (sides.at[1, first, :], west_ref.at[high, :]),
         (-1, -1): (sides.at[0, first, :], east_ref.at[high, :]),
     }, send_sems, recv_sems)
-    start_blocks, wait_blocks = swap_blocks(values_ref, observed_ref, far_send, far_recv, sems.at[4])
     start_halo()
-    start_blocks()
     for k in range(9):
         g = combined(corr_ref, jac_ref, k)
         hi, lo = split(g)
@@ -334,11 +287,9 @@
             gt_hi[half * 128:(half + 1) * 128, k * 128:(k + 1) * 128] = hi
             gt_lo[half * 128:(half + 1) * 128, k * 128:(k + 1) * 128] = lo
     wait_halo()
-    wait_blocks()
-
-
-def back_kernel(out_n, out_s, out_w, out_e, rounded_ref, got_n, got_s, got_w, got_e, nw, ne, sw, se, returned_ref,
-                send_sems, recv_sems, far_send, far_recv, own_sem):
+
+
+def back_kernel(out_n, out_s, out_w, out_e, got_n, got_s, got_w, got_e, nw, ne, sw, se, send_sems, recv_sems):
     cols = out_n.shape[0] - 2 * EDGE
     middle, low, high = pl.ds(EDGE, cols), pl.ds(0, EDGE), pl.ds(cols + EDGE, EDGE)
     greet()
@@ -352,11 +303,8 @@
         (-1, 1): (out_n.at[high, :], sw),
         (-1, -1): (out_n.at[low, :], se),
     }, send_sems, recv_sems)
-    start_blocks, wait_blocks = swap_blocks(rounded_ref, returned_ref, far_send, far_recv, own_sem)
     start_edges()
-    start_blocks()
     wait_edges()
-    wait_blocks()
 
 
 def finish_kernel(north_ref, south_ref, west_ref, east_ref, nw_ref, ne_ref, sw_ref, se_ref, grad_in,
@@ -398,31 +346,34 @@
     smem = pl.BlockSpec(memory_space=pltpu.SMEM)
     hbm = pl.BlockSpec(memory_space=pl.ANY)
 
+    def to_owners(x):
+        blocks = x.reshape(n_devices, CAP, channels)
+        return lax.all_to_all(blocks, ("lat", "lon"), split_axis=0, concat_axis=0, tiled=True).reshape(slots, channels)
+
+    observed = to_owners(obs_values)
+
     def struct(count):
         return jax.ShapeDtypeStruct((count, levels), F32)
 
-    north, south, west, east, observed, g_both, gt_hi, gt_lo = pl.pallas_call(
+    north, south, west, east, g_both, gt_hi, gt_lo = pl.pallas_call(
         front_kernel,
         out_shape=[struct(cols), struct(cols), struct(rows + 2 * EDGE), struct(rows + 2 * EDGE),
-                   jax.ShapeDtypeStruct((slots, channels), BF16),
                    jax.ShapeDtypeStruct((9 * levels, 2 * channels), BF16),
                    jax.ShapeDtypeStruct((2 * channels, 9 * levels), BF16),
                    jax.ShapeDtypeStruct((2 * channels, 9 * levels), BF16)],
-        in_specs=[hbm, hbm, vmem, vmem],
-        out_specs=[vmem] * 8,
+        in_specs=[hbm, vmem, vmem],
+        out_specs=[vmem] * 7,
         scratch_shapes=[
             pltpu.VMEM((2, rows, 8, levels), F32),
             pltpu.VMEM((2, cols, levels), F32),
             pltpu.VMEM((2, rows, levels), F32),
             pltpu.SemaphoreType.DMA((8,)),
             pltpu.SemaphoreType.DMA((8,)),
-            pltpu.SemaphoreType.DMA((5,)),
-            pltpu.SemaphoreType.DMA((n_devices,)),
-            pltpu.SemaphoreType.DMA((n_devices,)),
+            pltpu.SemaphoreType.DMA((4,)),
         ],
         compiler_params=pltpu.CompilerParams(collective_id=0, has_side_effects=True, vmem_limit_bytes=56 * 2**20),
         name="front",
-    )(control, obs_values, corr_blocks, jacobian)
+    )(control, corr_blocks, jacobian)
 
     chunk_slots = math.gcd(slots, 512)
     limit = pltpu.CompilerParams(vmem_limit_bytes=56 * 2**20)
@@ -433,7 +384,10 @@
         out_specs=[vmem, vmem],
         scratch_shapes=[
             pltpu.VMEM((rows + 2, pitch, levels), F32),
-            pltpu.VMEM((ODD * chunk_slots, levels), F32),
+            pltpu.VMEM((ODD * 8, levels), F32),
+            pltpu.VMEM((ODD * 8, levels), F32),
+            pltpu.VMEM((chunk_slots, levels), F32),
+            pltpu.VMEM((chunk_slots, levels), F32),
             pltpu.VMEM((2 * chunk_slots, 9 * levels), BF16),
             pltpu.SemaphoreType.DMA,
         ],
@@ -441,6 +395,8 @@
         cost_estimate=pl.CostEstimate(flops=2 * slots * 1152 * 512, bytes_accessed=40 * 2**20, transcendentals=0),
         name="forward",
     )(obs_col, obs_count, obs_frac, obs_rinv, observed, g_both, north, south, west, east, control)
+
+    returned = to_owners(rounded)
 
     gradient, out_n, out_s, out_w, out_e = pl.pallas_call(
         functools.partial(adjoint_kernel, pitch, chunk_slots),
@@ -455,7 +411,10 @@
         out_specs=[hbm] + [vmem] * 4,
         scratch_shapes=[
             pltpu.VMEM((rows + 2, pitch, levels), F32),
-            pltpu.VMEM((ODD * chunk_slots, levels), F32),
+            pltpu.VMEM((ODD * 8, levels), F32),
+            pltpu.VMEM((ODD * 8, levels), F32),
+            pltpu.VMEM((chunk_slots, levels), F32),
+            pltpu.VMEM((chunk_slots, levels), F32),
             pltpu.VMEM((chunk_slots, 9 * levels), F32),
             pltpu.SemaphoreType.DMA,
         ],
@@ -464,22 +423,18 @@
         name="adjoint",
     )(obs_col, obs_frac, gt_hi, gt_lo, weighted, control)
 
-    *got, returned = pl.pallas_call(
+    got = pl.pallas_call(
         back_kernel,
-        out_shape=[struct(cols), struct(cols), struct(rows), struct(rows)] + [struct(EDGE)] * 4
-        + [jax.ShapeDtypeStruct((slots, channels), BF16)],
-        in_specs=[vmem] * 4 + [hbm],
-        out_specs=[vmem] * 9,
+        out_shape=[struct(cols), struct(cols), struct(rows), struct(rows)] + [struct(EDGE)] * 4,
+        in_specs=[vmem] * 4,
+        out_specs=[vmem] * 8,
         scratch_shapes=[
             pltpu.SemaphoreType.DMA((8,)),
             pltpu.SemaphoreType.DMA((8,)),
-            pltpu.SemaphoreType.DMA((n_devices,)),
-            pltpu.SemaphoreType.DMA((n_devices,)),
-            pltpu.SemaphoreType.DMA,
         ],
         compiler_params=pltpu.CompilerParams(collective_id=1, has_side_effects=True),
         name="back",
-    )(out_n, out_s, out_w, out_e, rounded)
+    )(out_n, out_s, out_w, out_e)
     gradient = pl.pallas_call(
         finish_kernel,
         out_shape=jax.ShapeDtypeStruct(control.shape, F32),

time: 95.1 us -> 82.9 us (0.87)
  Pallas kernels: 93.2 us -> 63.4 us
  starting transfers between devices: 0 us -> 11.7 us
  waiting for transfers between devices: 0 us -> 4.76 us
    pallas_call x1, Pallas kernels: 24.2 us -> 11.6 us  [body(): pl.pallas_call(front_kernel, out_shape=[struct(cols), struct(cols), struc...]
    pallas_call x1, Pallas kernels: 19.9 us -> 8.13 us  [body(): pl.pallas_call(back_kernel, out_shape=[struct(cols), struct(cols), struct...]
    all_to_all x0 -> x2, starting transfers between devices: none -> 11.7 us  [to_owners(): lax.all_to_all(blocks, ('lat', 'lon'), split_axis=0, concat_axis=0, tiled...]
    all_to_all x0 -> x2, waiting for transfers between devices: none -> 4.76 us  [to_owners(): lax.all_to_all(blocks, ('lat', 'lon'), split_axis=0, concat_axis=0, tiled...]
    pallas_call x1, Pallas kernels: 21.1 us -> 16.7 us  [body(): pl.pallas_call(functools.partial(forward_kernel, pitch, chunk_slots), out...]
    pallas_call x1, Pallas kernels: 24.7 us -> 23.7 us  [body(): pl.pallas_call(functools.partial(adjoint_kernel, pitch, chunk_slots), out...]
  transfers between devices with their start and end apart: 0 -> 2, of which waited for: 0 -> 1; matrix products, arithmetic and copies ran while one was open for 0% -> 0% of each run, Pallas kernels for 0% -> 57%
where the time goes in v4:
time: 82.9 us; the launch traced here: 82.1 us
  Pallas kernels  63.4 us (76%)
  starting transfers between devices  11.7 us (14%)
  waiting for transfers between devices  4.76 us (6%)
  local copies, waits for them, and re-layouts  1.59 us (2%)
    pallas_call x1, Pallas kernels, body(): pl.pallas_call(functools.partial(adjoint_kernel, pitch, chunk_slots), out...  23.7 us
    pallas_call x1, Pallas kernels, body(): pl.pallas_call(functools.partial(forward_kernel, pitch, chunk_slots), out...  16.7 us
    all_to_all x2, starting transfers between devices, to_owners(): lax.all_to_all(blocks, ('lat', 'lon'), split_axis=0, concat_axis=0, tiled...  11.7 us
    pallas_call x1, Pallas kernels, body(): pl.pallas_call(front_kernel, out_shape=[struct(cols), struct(cols), struc...  11.6 us
    pallas_call x1, Pallas kernels, body(): pl.pallas_call(back_kernel, out_shape=[struct(cols), struct(cols), struct...  8.13 us
    all_to_all x2, waiting for transfers between devices, to_owners(): lax.all_to_all(blocks, ('lat', 'lon'), split_axis=0, concat_axis=0, tiled...  4.76 us
    pallas_call x1, Pallas kernels, body(): pl.pallas_call(finish_kernel, out_shape=jax.ShapeDtypeStruct(control.shap...  3.28 us
  transfers between devices with their start and end apart: 2, of which 1 were waited for; matrix products, arithmetic and copies ran while one was open for 0% of the time, Pallas kernels for 57%

profile of v4, /device:TPU:0, one launch (start us, length us, event | category | flops | bytes accessed | tf_op | source)
XLA Modules:
  0.0 82.1 jit_solution(5212956390887448960)
XLA Ops:
  0.6 7.3 %all-to-all-start = ((bf16[32,64,128]{2,1,0:T(8,128)(2,1)}), bf16[32,64,128]{2,1,0:T(8,128)(2,1)S(1)}, u32[]{:S(2)}, u32[]{:S(2)}) async-start(bf16[32,64,128]{2,1,0:T(8,128)(2,1)} %bitcast.6), calls=%async_computation | async-start | bytes 1048576 | tf_op jit(solution)/shard_map/all_to_all | solution.py:351
  7.9 11.6 %front.1 = (f32[128,128]{1,0:T(8,128)}, f32[128,128]{1,0:T(8,128)}, f32[144,128]{1,0:T(8,128)}, f32[144,128]{1,0:T(8,128)}, bf16[1152,256]{1,0:T(8,128)(2,1)}, /...) custom-call(f32[128,128,128]{2,1,0:T(8,128)} %control_ref.5, f32[9,128,128]{2,1,0:T(8,128)} %corr_ref.1, ...), custom_call_target="tpu_custom_call" | custom-call | tf_op jit(solution)/shard_map/front/pallas_call | solution.py:358
  19.5 4.8 %all-to-all-done = bf16[32,64,128]{2,1,0:T(8,128)(2,1)S(1)} async-done(((bf16[32,64,128]{2,1,0:T(8,128)(2,1)}), bf16[32,64,128]{2,1,0:T(8,128)(2,1)S(1)}, u32[]{:S(2)}, u32[]{:S(2)}) %all-to-all-start) | async-done | bytes 524320 | tf_op jit(solution)/shard_map/all_to_all | solution.py:351
  24.3 0.0 copy-start
  24.3 0.8 copy-done
  25.1 16.7 %forward.1 = (f32[2048,128]{1,0:T(8,128)}, bf16[2048,128]{1,0:T(8,128)(2,1)}) custom-call(s32[1,2048]{1,0:T(1,128)} %col_ref.3, s32[1,32]{1,0:T(1,128)} %count_ref.1, f32[1,2,2048]{2,1,0:T(2,128)} %frac_ref.3, f32[1,2048]{1,0:T(1,128)} %rinv_ref.1, bf16[2048,128]{1,0:T(8,128)(2,1)} %bitcast.4, bf16[1152,256]{1,0:T(8,128)(2,1)} %get-tuple-element.26.g_both, ...), custom_call_target="tpu_custom_call" | custom-call | flops 2415919104 | bytes 41943040 | tf_op jit(solution)/shard_map/forward/pallas_call | solution.py:380
  41.8 4.4 %all-to-all-start.1 = ((bf16[32,64,128]{2,1,0:T(8,128)(2,1)}), bf16[32,64,128]{2,1,0:T(8,128)(2,1)S(1)}, u32[]{:S(2)}, u32[]{:S(2)}) async-start(bf16[32,64,128]{2,1,0:T(8,128)(2,1)} %bitcast.7), calls=%async_computation.1 | async-start | bytes 1048576 | tf_op jit(solution)/shard_map/all_to_all | solution.py:351
  46.2 23.7 %adjoint.1 = (f32[128,128,128]{2,1,0:T(8,128)}, f32[144,128]{1,0:T(8,128)}, f32[144,128]{1,0:T(8,128)}, f32[128,128]{1,0:T(8,128)}, f32[128,128]{1,0:T(8,128)}) custom-call(s32[1,2048]{1,0:T(1,128)} %col_ref.3, f32[1,2,2048]{2,1,0:T(2,128)} %frac_ref.3, bf16[256,1152]{1,0:T(8,128)(2,1)} %get-tuple-element.24.gt_hi, ...), custom_call_target="tpu_custom_call" | custom-call | flops 2415919104 | bytes 62914560 | tf_op jit(solution)/shard_map/adjoint/pallas_call | solution.py:401
  69.9 8.1 %back.1 = (f32[128,128]{1,0:T(8,128)}, f32[128,128]{1,0:T(8,128)}, f32[128,128]{1,0:T(8,128)}, f32[128,128]{1,0:T(8,128)}, f32[8,128]{1,0:T(8,128)}, /*index=5*/...) custom-call(f32[144,128]{1,0:T(8,128)} %get-tuple-element.32.out_n, f32[144,128]{1,0:T(8,128)} %get-tuple-element.33.out_s, ...), custom_call_target="tpu_custom_call" | custom-call | tf_op jit(solution)/shard_map/back/pallas_call | solution.py:426
  78.0 3.3 %finish.1 = f32[128,128,128]{2,1,0:T(8,128)} custom-call(f32[128,128]{1,0:T(8,128)} %get-tuple-element.36.north_ref, f32[128,128]{1,0:T(8,128)} %get-tuple-element.37.south_ref, f32[128,128]{1,0:T(8,128)} %get-tuple-element.38.west_ref, f32[128,128]{1,0:T(8,128)} %get-tuple-element.39.east_ref, ...), custom_call_target="tpu_custom_call", output_to_operand_aliasing={{}: (8, {})} | custom-call | tf_op jit(solution)/shard_map/finish/pallas_call | solution.py:438
  81.3 0.0 all-to-all-done.1
  81.3 0.8 copy.13
Async XLA Ops:
  0.6 23.7 %all-to-all-start = ((bf16[32,64,128]{2,1,0:T(8,128)(2,1)}), bf16[32,64,128]{2,1,0:T(8,128)(2,1)S(1)}, u32[]{:S(2)}, u32[]{:S(2)}) async-start(bf16[32,64,128]{2,1,0:T(8,128)(2,1)} %bitcast.6), calls=%async_computation | async-start | bytes 1048576 | tf_op jit(solution)/shard_map/all_to_all | solution.py:351
  24.3 0.8 copy-start
  41.8 39.5 %all-to-all-start.1 = ((bf16[32,64,128]{2,1,0:T(8,128)(2,1)}), bf16[32,64,128]{2,1,0:T(8,128)(2,1)S(1)}, u32[]{:S(2)}, u32[]{:S(2)}) async-start(bf16[32,64,128]{2,1,0:T(8,128)(2,1)} %bitcast.7), calls=%async_computation.1 | async-start | bytes 1048576 | tf_op jit(solution)/shard_map/all_to_all | solution.py:351

commit v5 on v4

--- a/solution.py
+++ b/solution.py
@@ -10,6 +10,7 @@
 CAP = 64
 SUB = 128
 ODD = 17
+CLASH = 1 << 20
 EDGE = 8
 F32 = jnp.float32
 BF16 = jnp.bfloat16
@@ -29,16 +30,36 @@
     return jnp.dot(corr_ref[k], jac_ref[...], precision=lax.Precision.HIGHEST, preferred_element_type=F32)
 
 
-def place(corner, cols, pitch):
-    if cols & (cols - 1) == 0:
-        line = lax.shift_right_logical(corner, cols.bit_length() - 1)
-    else:
-        line = lax.div(corner, cols)
-    return corner + line * (pitch - cols) + (EDGE - 1)
-
-
-def forward_kernel(pitch, chunk_slots, col_ref, count_ref, frac_ref, rinv_ref, observed_ref, g_both,
-                   north_ref, south_ref, west_ref, east_ref, control_ref, weighted_ref, rounded_ref,
+def entries_of(corner, cols, pitch):
+    i, j = corner // cols, corner % cols
+    slot = lax.broadcasted_iota(jnp.int32, corner.shape, 1) % 8
+    clash = jnp.zeros(corner.shape, jnp.bool_)
+    for k in range(1, 8):
+        near = (jnp.abs(i - jnp.roll(i, k, axis=1)) < 4) & (jnp.abs(j - jnp.roll(j, k, axis=1)) < 4)
+        clash |= near & (slot >= k)
+    return i * pitch + j + (EDGE - 1) + jnp.where(clash, CLASH, 0)
+
+
+def weigh_kernel(count_ref, rinv_ref, observed_ref, evolved_ref, weighted_ref, rounded_ref):
+    lane = lax.broadcasted_iota(jnp.int32, (1, SUB), 1)
+
+    def part(m, c):
+        at = pl.ds(pl.multiple_of(m * SUB, SUB), SUB)
+        live = jnp.zeros((1, SUB), jnp.int32)
+        for n in range(SUB // CAP):
+            count = count_ref[0, m * (SUB // CAP) + n]
+            live += ((lane >= n * CAP) & (lane < n * CAP + count)).astype(jnp.int32)
+        rinv = jnp.where(live > 0, rinv_ref[0:1, at], 0.0)
+        weighted = column(rinv) * (evolved_ref[at, :] - observed_ref[at, :].astype(F32))
+        weighted_ref[at, :] = weighted
+        rounded_ref[at, :] = weighted.astype(BF16)
+        return c
+
+    lax.fori_loop(0, evolved_ref.shape[0] // SUB, part, 0)
+
+
+def forward_kernel(pitch, chunk_slots, entry_ref, frac_ref, g_both,
+                   north_ref, south_ref, west_ref, east_ref, control_ref, evolved_ref,
                    pad, patches_a, patches_b, f_ref, g_ref, p_both, sem):
     rows, cols, _ = control_ref.shape
     fetch = pltpu.make_async_copy(control_ref, pad.at[pl.ds(1, rows), pl.ds(EDGE, cols), :], sem)
@@ -60,7 +81,7 @@
 
         def pick(start, patches):
             for v in range(8):
-                base = place(col_ref[0, first + start + v], cols, pitch)
+                base = entry_ref[0, first + start + v] & (CLASH - 1)
                 for r in range(4):
                     patches[v * ODD + r * 4:v * ODD + r * 4 + 4, :] = flat[pl.ds(base + r * pitch, 4), :]
 
@@ -93,24 +114,14 @@
         both = jnp.dot(p_both[...], g_both[...], preferred_element_type=F32)
         for m in range(chunk_slots // SUB):
             hi, lo = both[m * SUB:(m + 1) * SUB], both[chunk_slots + m * SUB:chunk_slots + (m + 1) * SUB]
-            evolved = hi[:, 0:128] + (hi[:, 128:256] + lo[:, 0:128] + lo[:, 128:256])
-            start = pl.multiple_of(first + m * SUB, SUB)
-            at = pl.ds(start, SUB)
-            lane = lax.broadcasted_iota(jnp.int32, (1, SUB), 1)
-            live = jnp.zeros((1, SUB), jnp.int32)
-            for part in range(SUB // CAP):
-                count = count_ref[0, n * (chunk_slots // CAP) + m * (SUB // CAP) + part]
-                live += ((lane >= part * CAP) & (lane < part * CAP + count)).astype(jnp.int32)
-            rinv = jnp.where(live > 0, rinv_ref[0:1, at], 0.0)
-            weighted = column(rinv) * (evolved - observed_ref[at, :].astype(F32))
-            weighted_ref[at, :] = weighted
-            rounded_ref[at, :] = weighted.astype(BF16)
+            at = pl.ds(pl.multiple_of(first + m * SUB, SUB), SUB)
+            evolved_ref[at, :] = hi[:, 0:128] + (hi[:, 128:256] + lo[:, 0:128] + lo[:, 128:256])
         return carry
 
-    lax.fori_loop(0, col_ref.shape[1] // chunk_slots, chunk, 0)
-
-
-def adjoint_kernel(pitch, chunk_slots, col_ref, frac_ref, gt_hi, gt_lo, weighted_ref, control_ref,
+    lax.fori_loop(0, entry_ref.shape[1] // chunk_slots, chunk, 0)
+
+
+def adjoint_kernel(pitch, chunk_slots, entry_ref, frac_ref, gt_hi, gt_lo, weighted_ref, control_ref,
                    grad_ref, north_ref, south_ref, west_ref, east_ref, pad, patches_a, patches_b, f_ref, g_ref, q_ref, sem):
     rows, cols, _ = control_ref.shape
     inner = pad.at[pl.ds(1, rows), pl.ds(EDGE, cols), :]
@@ -154,27 +165,42 @@
                     terms = ([rest_f * line[r]] if r < 3 else []) + ([f * line[r - 1]] if r > 0 else [])
                     patches[pl.ds(r * 4 + c, 8, stride=ODD), :] = sum(terms[1:], terms[0])
 
-        def spread(start, patches):
-            for v in range(8):
-                base = place(col_ref[0, first + start + v], cols, pitch)
-                lines = [flat[pl.ds(base + r * pitch, 4), :] + patches[v * ODD + r * 4:v * ODD + r * 4 + 4, :]
-                         for r in range(4)]
-                for r in range(4):
-                    flat[pl.ds(base + r * pitch, 4), :] = lines[r]
+        def spread(entries, patches, apart):
+            def summed(v):
+                base = entries[v] & (CLASH - 1)
+                return [(pl.ds(base + r * pitch, 4),
+                         flat[pl.ds(base + r * pitch, 4), :] + patches[v * ODD + r * 4:v * ODD + r * 4 + 4, :])
+                        for r in range(4)]
+
+            for group in ([range(8)] if apart else [[v] for v in range(8)]):
+                for where, value in [one for v in group for one in summed(v)]:
+                    flat[where, :] = value
+
+        def step(start, patches, later, later_patches):
+            entries = [entry_ref[0, first + start + v] for v in range(8)]
+            clash = functools.reduce(lambda x, y: x | y, entries) >= CLASH
+
+            @pl.when(jnp.logical_not(clash))
+            def _():
+                spread(entries, patches, True)
+                mix(later, later_patches)
+
+            @pl.when(clash)
+            def _():
+                spread(entries, patches, False)
+                mix(later, later_patches)
 
         def pair(t, c):
             start = t * 16
-            mix(start + 8, patches_b)
-            spread(start, patches_a)
-            mix(jnp.minimum(start + 16, chunk_slots - 8), patches_a)
-            spread(start + 8, patches_b)
+            step(start, patches_a, start + 8, patches_b)
+            step(start + 8, patches_b, jnp.minimum(start + 16, chunk_slots - 8), patches_a)
             return c
 
         mix(0, patches_a)
-        lax.fori_loop(0, chunk_slots // 16, pair, 0, unroll=2)
+        lax.fori_loop(0, chunk_slots // 16, pair, 0)
         return carry
 
-    lax.fori_loop(0, col_ref.shape[1] // chunk_slots, chunk, 0)
+    lax.fori_loop(0, entry_ref.shape[1] // chunk_slots, chunk, 0)
     send = pltpu.make_async_copy(inner, grad_ref, sem)
     send.start()
     north_ref[...] = pad[0]
@@ -377,11 +403,12 @@
 
     chunk_slots = math.gcd(slots, 512)
     limit = pltpu.CompilerParams(vmem_limit_bytes=56 * 2**20)
-    weighted, rounded = pl.pallas_call(
+    entries = entries_of(obs_col, cols, pitch)
+    evolved = pl.pallas_call(
         functools.partial(forward_kernel, pitch, chunk_slots),
-        out_shape=[jax.ShapeDtypeStruct((slots, channels), F32), jax.ShapeDtypeStruct((slots, channels), BF16)],
-        in_specs=[smem, smem] + [vmem] * 8 + [hbm],
-        out_specs=[vmem, vmem],
+        out_shape=jax.ShapeDtypeStruct((slots, channels), F32),
+        in_specs=[smem] + [vmem] * 6 + [hbm],
+        out_specs=vmem,
         scratch_shapes=[
             pltpu.VMEM((rows + 2, pitch, levels), F32),
             pltpu.VMEM((ODD * 8, levels), F32),
@@ -394,7 +421,16 @@
         compiler_params=limit,
         cost_estimate=pl.CostEstimate(flops=2 * slots * 1152 * 512, bytes_accessed=40 * 2**20, transcendentals=0),
         name="forward",
-    )(obs_col, obs_count, obs_frac, obs_rinv, observed, g_both, north, south, west, east, control)
+    )(entries, obs_frac, g_both, north, south, west, east, control)
+
+    weighted, rounded = pl.pallas_call(
+        weigh_kernel,
+        out_shape=[jax.ShapeDtypeStruct((slots, channels), F32), jax.ShapeDtypeStruct((slots, channels), BF16)],
+        in_specs=[smem] + [vmem] * 3,
+        out_specs=[vmem, vmem],
+        compiler_params=limit,
+        name="weigh",
+    )(obs_count, obs_rinv, observed, evolved)
 
     returned = to_owners(rounded)
 
@@ -421,7 +457,7 @@
         compiler_params=limit,
         cost_estimate=pl.CostEstimate(flops=2 * slots * 1152 * 512, bytes_accessed=60 * 2**20, transcendentals=0),
         name="adjoint",
-    )(obs_col, obs_frac, gt_hi, gt_lo, weighted, control)
+    )(entries, obs_frac, gt_hi, gt_lo, weighted, control)
 
     got = pl.pallas_call(
         back_kernel,

time: 82.9 us -> 89.2 us (1.076)
  waiting for transfers between devices: 4.76 us -> 0.01 us
  other arithmetic: 0 us -> 3.68 us
  starting transfers between devices: 11.7 us -> 15 us
  local copies, waits for them, and re-layouts: 1.59 us -> 3.61 us
  Pallas kernels: 63.4 us -> 65.2 us
    all_to_all x2, waiting for transfers between devices: 4.76 us -> 0.01 us  [to_owners(): lax.all_to_all(blocks, ('lat', 'lon'), split_axis=0, concat_axis=0, tiled...]
    pallas_call x0 -> x1, Pallas kernels: none -> 4.35 us  [body(): pl.pallas_call(weigh_kernel, out_shape=[jax.ShapeDtypeStruct((slots, chan...]
    all_to_all x2, starting transfers between devices: 11.7 us -> 15 us  [to_owners(): lax.all_to_all(blocks, ('lat', 'lon'), split_axis=0, concat_axis=0, tiled...]
    add x0 -> x1, other arithmetic: none -> 2.22 us  [entries_of(): return i * pitch + j + (EDGE - 1) + jnp.where(clash, CLASH, 0)]
    pallas_call x1, Pallas kernels: 11.6 us -> 9.53 us  [body(): pl.pallas_call(front_kernel, out_shape=[struct(cols), struct(cols), struc...]
    slice x0 -> x14, local copies, waits for them, and re-layouts: none -> 2.02 us  [the longest x7 1.01 us: entries_of(): jnp.roll(i, k, axis=1)]
    select_n x0 -> x2, other arithmetic: none -> 1.46 us  [entries_of(): i, j = (corner // cols, corner % cols)]
  transfers between devices with their start and end apart: 2 -> 2, of which waited for: 1 -> 0; matrix products, arithmetic and copies ran while one was open for 0% -> 6% of each run, Pallas kernels for 57% -> 69%
where the time goes in v5:
time: 89.2 us; the launch traced here: 88.2 us
  Pallas kernels  65.2 us (73%)
  starting transfers between devices  15 us (17%)
  other arithmetic  3.68 us (4%)
  local copies, waits for them, and re-layouts  3.61 us (4%)
    pallas_call x1, Pallas kernels, body(): pl.pallas_call(functools.partial(adjoint_kernel, pitch, chunk_slots), out...  24 us
    pallas_call x1, Pallas kernels, body(): pl.pallas_call(functools.partial(forward_kernel, pitch, chunk_slots), out...  15.9 us
    all_to_all x2, starting transfers between devices, to_owners(): lax.all_to_all(blocks, ('lat', 'lon'), split_axis=0, concat_axis=0, tiled...  15 us
    pallas_call x1, Pallas kernels, body(): pl.pallas_call(front_kernel, out_shape=[struct(cols), struct(cols), struc...  9.53 us
    pallas_call x1, Pallas kernels, body(): pl.pallas_call(back_kernel, out_shape=[struct(cols), struct(cols), struct...  8.13 us
    pallas_call x1, Pallas kernels, body(): pl.pallas_call(weigh_kernel, out_shape=[jax.ShapeDtypeStruct((slots, chan...  4.35 us
    pallas_call x1, Pallas kernels, body(): pl.pallas_call(finish_kernel, out_shape=jax.ShapeDtypeStruct(control.shap...  3.28 us
    add x1, other arithmetic, entries_of(): return i * pitch + j + (EDGE - 1) + jnp.where(clash, CLASH, 0)  2.22 us
  transfers between devices with their start and end apart: 2, of which 0 were waited for; matrix products, arithmetic and copies ran while one was open for 6% of the time, Pallas kernels for 69%

profile of v5, /device:TPU:0, one launch (start us, length us, event | category | flops | bytes accessed | tf_op | source)
XLA Modules:
  0.0 88.2 jit_solution(1816996247568651532)
XLA Ops:
  0.6 7.3 %all-to-all-start = ((bf16[32,64,128]{2,1,0:T(8,128)(2,1)}), bf16[32,64,128]{2,1,0:T(8,128)(2,1)S(1)}, u32[]{:S(2)}, u32[]{:S(2)}) async-start(bf16[32,64,128]{2,1,0:T(8,128)(2,1)} %bitcast.34), calls=%async_computation | async-start | bytes 1048576 | tf_op jit(solution)/shard_map/all_to_all | solution.py:377
  7.9 0.7 and_select_fusion.1
  8.7 0.6 slice.128
  9.3 0.1 slice.144
  9.3 0.1 slice.152
  9.4 0.1 slice.140
  9.5 0.1 slice.148
  9.6 0.1 slice.132
  9.7 0.7 and_select_fusion.2
  10.4 0.6 slice.126
  11.0 0.1 slice.142
  11.1 0.1 slice.150
  11.1 0.1 slice.138
  11.2 0.1 slice.134
  11.4 9.5 %front.1 = (f32[128,128]{1,0:T(8,128)}, f32[128,128]{1,0:T(8,128)}, f32[144,128]{1,0:T(8,128)}, f32[144,128]{1,0:T(8,128)}, bf16[1152,256]{1,0:T(8,128)(2,1)}, /...) custom-call(f32[128,128,128]{2,1,0:T(8,128)} %control_ref.5, f32[9,128,128]{2,1,0:T(8,128)} %corr_ref.1, ...), custom_call_target="tpu_custom_call" | custom-call | tf_op jit(solution)/shard_map/front/pallas_call | solution.py:384
  21.0 2.2 %add_add_fusion.entry_ref = s32[1,2048]{1,0:T(1,128)} fusion(s32[1,2048]{1,0:T(1,128)S(1)} %and_select_fusion.2, s32[1,2041]{1,0:T(1,128)S(1)} %bitcast.27, s32[1,7]{1,0:T(1,128)S(1)} %slice.152, s32[1,2041]{1,0:T(1,128)S(1)} %bitcast.20, s32[1,7]{1,0:T(1,128)S(1)} %slice.150, s32[1,2042]{1,0:T(1,128)S(1)} %bitcast.28, s32[1,6]{1,0:T(1,128)S(1)} %slice.148, ...), kind=kLoop, calls=%fused_computation.35 | loop fusion | flops 202752 | bytes 139264 | tf_op jit(solution)/shard_map/add | solution.py:40
  23.2 15.9 %forward.1.evolved_ref = f32[2048,128]{1,0:T(8,128)} custom-call(s32[1,2048]{1,0:T(1,128)} %add_add_fusion.entry_ref, f32[1,2,2048]{2,1,0:T(2,128)} %frac_ref.3, bf16[1152,256]{1,0:T(8,128)(2,1)} %get-tuple-element.26.g_both, f32[128,128]{1,0:T(8,128)} %get-tuple-element.27.north_ref, f32[128,128]{1,0:T(8,128)} %get-tuple-element.28.south_ref, ...), custom_call_target="tpu_custom_call" | custom-call | flops 2415919104 | bytes 41943040 | tf_op jit(solution)/shard_map/forward/pallas_call | solution.py:407
  39.1 0.8 copy-done
  39.9 4.4 %weigh.1 = (f32[2048,128]{1,0:T(8,128)}, bf16[2048,128]{1,0:T(8,128)(2,1)}) custom-call(s32[1,32]{1,0:T(1,128)} %count_ref.1, f32[1,2048]{1,0:T(1,128)} %rinv_ref.1, bf16[2048,128]{1,0:T(8,128)(2,1)} %bitcast.18, f32[2048,128]{1,0:T(8,128)} %forward.1.evolved_ref), custom_call_target="tpu_custom_call" | custom-call | tf_op jit(solution)/shard_map/weigh/pallas_call | solution.py:426
  44.3 7.7 %all-to-all-start.1 = ((bf16[32,64,128]{2,1,0:T(8,128)(2,1)}), bf16[32,64,128]{2,1,0:T(8,128)(2,1)S(1)}, u32[]{:S(2)}, u32[]{:S(2)}) async-start(bf16[32,64,128]{2,1,0:T(8,128)(2,1)} %bitcast.35), calls=%async_computation.1 | async-start | bytes 1048576 | tf_op jit(solution)/shard_map/all_to_all | solution.py:377
  51.9 24.0 %adjoint.1 = (f32[128,128,128]{2,1,0:T(8,128)}, f32[144,128]{1,0:T(8,128)}, f32[144,128]{1,0:T(8,128)}, f32[128,128]{1,0:T(8,128)}, f32[128,128]{1,0:T(8,128)}) custom-call(s32[1,2048]{1,0:T(1,128)} %add_add_fusion.entry_ref, f32[1,2,2048]{2,1,0:T(2,128)} %frac_ref.3, bf16[256,1152]{1,0:T(8,128)(2,1)} %get-tuple-element.24.gt_hi, ...), custom_call_target="tpu_custom_call" | custom-call | flops 2415919104 | bytes 62914560 | tf_op jit(solution)/shard_map/adjoint/pallas_call | solution.py:437
  75.9 8.1 %back.1 = (f32[128,128]{1,0:T(8,128)}, f32[128,128]{1,0:T(8,128)}, f32[128,128]{1,0:T(8,128)}, f32[128,128]{1,0:T(8,128)}, f32[8,128]{1,0:T(8,128)}, /*index=5*/...) custom-call(f32[144,128]{1,0:T(8,128)} %get-tuple-element.32.out_n, f32[144,128]{1,0:T(8,128)} %get-tuple-element.33.out_s, ...), custom_call_target="tpu_custom_call" | custom-call | tf_op jit(solution)/shard_map/back/pallas_call | solution.py:462
  84.1 3.3 %finish.1 = f32[128,128,128]{2,1,0:T(8,128)} custom-call(f32[128,128]{1,0:T(8,128)} %get-tuple-element.36.north_ref, f32[128,128]{1,0:T(8,128)} %get-tuple-element.37.south_ref, f32[128,128]{1,0:T(8,128)} %get-tuple-element.38.west_ref, f32[128,128]{1,0:T(8,128)} %get-tuple-element.39.east_ref, ...), custom_call_target="tpu_custom_call", output_to_operand_aliasing={{}: (8, {})} | custom-call | tf_op jit(solution)/shard_map/finish/pallas_call | solution.py:474
  87.4 0.8 copy.13
  (6 shorter events, 0.2 us)
Async XLA Ops:
  0.6 38.5 %all-to-all-start = ((bf16[32,64,128]{2,1,0:T(8,128)(2,1)}), bf16[32,64,128]{2,1,0:T(8,128)(2,1)S(1)}, u32[]{:S(2)}, u32[]{:S(2)}) async-start(bf16[32,64,128]{2,1,0:T(8,128)(2,1)} %bitcast.34), calls=%async_computation | async-start | bytes 1048576 | tf_op jit(solution)/shard_map/all_to_all | solution.py:377
  39.1 0.8 copy-start
  44.3 43.1 %all-to-all-start.1 = ((bf16[32,64,128]{2,1,0:T(8,128)(2,1)}), bf16[32,64,128]{2,1,0:T(8,128)(2,1)S(1)}, u32[]{:S(2)}, u32[]{:S(2)}) async-start(bf16[32,64,128]{2,1,0:T(8,128)(2,1)} %bitcast.35), calls=%async_computation.1 | async-start | bytes 1048576 | tf_op jit(solution)/shard_map/all_to_all | solution.py:377

commit v6 on v4

--- a/solution.py
+++ b/solution.py
@@ -37,8 +37,8 @@
     return corner + line * (pitch - cols) + (EDGE - 1)
 
 
-def forward_kernel(pitch, chunk_slots, col_ref, count_ref, frac_ref, rinv_ref, observed_ref, g_both,
-                   north_ref, south_ref, west_ref, east_ref, control_ref, weighted_ref, rounded_ref,
+def forward_kernel(pitch, chunk_slots, col_ref, frac_ref, g_both,
+                   north_ref, south_ref, west_ref, east_ref, control_ref, evolved_ref,
                    pad, patches_a, patches_b, f_ref, g_ref, p_both, sem):
     rows, cols, _ = control_ref.shape
     fetch = pltpu.make_async_copy(control_ref, pad.at[pl.ds(1, rows), pl.ds(EDGE, cols), :], sem)
@@ -93,18 +93,8 @@
         both = jnp.dot(p_both[...], g_both[...], preferred_element_type=F32)
         for m in range(chunk_slots // SUB):
             hi, lo = both[m * SUB:(m + 1) * SUB], both[chunk_slots + m * SUB:chunk_slots + (m + 1) * SUB]
-            evolved = hi[:, 0:128] + (hi[:, 128:256] + lo[:, 0:128] + lo[:, 128:256])
-            start = pl.multiple_of(first + m * SUB, SUB)
-            at = pl.ds(start, SUB)
-            lane = lax.broadcasted_iota(jnp.int32, (1, SUB), 1)
-            live = jnp.zeros((1, SUB), jnp.int32)
-            for part in range(SUB // CAP):
-                count = count_ref[0, n * (chunk_slots // CAP) + m * (SUB // CAP) + part]
-                live += ((lane >= part * CAP) & (lane < part * CAP + count)).astype(jnp.int32)
-            rinv = jnp.where(live > 0, rinv_ref[0:1, at], 0.0)
-            weighted = column(rinv) * (evolved - observed_ref[at, :].astype(F32))
-            weighted_ref[at, :] = weighted
-            rounded_ref[at, :] = weighted.astype(BF16)
+            at = pl.ds(pl.multiple_of(first + m * SUB, SUB), SUB)
+            evolved_ref[at, :] = hi[:, 0:128] + (hi[:, 128:256] + lo[:, 0:128] + lo[:, 128:256])
         return carry
 
     lax.fori_loop(0, col_ref.shape[1] // chunk_slots, chunk, 0)
@@ -125,7 +115,6 @@
         return c
 
     lax.fori_loop(1, rows + 1, clear, 0)
-    fetch.wait()
     flat = pad.reshape((rows + 2) * pitch, 128)
 
     def chunk(n, carry):
@@ -171,6 +160,11 @@
             return c
 
         mix(0, patches_a)
+
+        @pl.when(n == 0)
+        def _():
+            fetch.wait()
+
         lax.fori_loop(0, chunk_slots // 16, pair, 0, unroll=2)
         return carry
 
@@ -377,11 +371,11 @@
 
     chunk_slots = math.gcd(slots, 512)
     limit = pltpu.CompilerParams(vmem_limit_bytes=56 * 2**20)
-    weighted, rounded = pl.pallas_call(
+    evolved = pl.pallas_call(
         functools.partial(forward_kernel, pitch, chunk_slots),
-        out_shape=[jax.ShapeDtypeStruct((slots, channels), F32), jax.ShapeDtypeStruct((slots, channels), BF16)],
-        in_specs=[smem, smem] + [vmem] * 8 + [hbm],
-        out_specs=[vmem, vmem],
+        out_shape=jax.ShapeDtypeStruct((slots, channels), F32),
+        in_specs=[smem] + [vmem] * 6 + [hbm],
+        out_specs=vmem,
         scratch_shapes=[
             pltpu.VMEM((rows + 2, pitch, levels), F32),
             pltpu.VMEM((ODD * 8, levels), F32),
@@ -394,7 +388,12 @@
         compiler_params=limit,
         cost_estimate=pl.CostEstimate(flops=2 * slots * 1152 * 512, bytes_accessed=40 * 2**20, transcendentals=0),
         name="forward",
-    )(obs_col, obs_count, obs_frac, obs_rinv, observed, g_both, north, south, west, east, control)
+    )(obs_col, obs_frac, g_both, north, south, west, east, control)
+
+    live = (jnp.arange(CAP, dtype=jnp.int32)[None, :] < obs_count[0][:, None]).reshape(slots, 1)
+    departure = evolved - observed.astype(F32)
+    weighted = jnp.where(live, obs_rinv[0][:, None] * departure, jnp.zeros_like(departure))
+    rounded = weighted.astype(BF16)
 
     returned = to_owners(rounded)
 

time: 82.9 us -> 83.6 us (level)
  waiting for transfers between devices: 4.76 us -> 0.01 us
  starting transfers between devices: 11.7 us -> 16.1 us
  other arithmetic: 0 us -> 3.35 us
  Pallas kernels: 63.4 us -> 61.6 us
    all_to_all x2, waiting for transfers between devices: 4.76 us -> 0.01 us  [to_owners(): lax.all_to_all(blocks, ('lat', 'lon'), split_axis=0, concat_axis=0, tiled...]
    all_to_all x2, starting transfers between devices: 11.7 us -> 16.1 us  [to_owners(): lax.all_to_all(blocks, ('lat', 'lon'), split_axis=0, concat_axis=0, tiled...]
    convert_element_type x0 -> x1, other arithmetic: none -> 2.62 us  [body(): rounded = weighted.astype(BF16)]
    pallas_call x1, Pallas kernels: 23.7 us -> 22.8 us  [body(): pl.pallas_call(functools.partial(adjoint_kernel, pitch, chunk_slots), out...]
  transfers between devices with their start and end apart: 2 -> 2, of which waited for: 1 -> 0; matrix products, arithmetic and copies ran while one was open for 0% -> 1% of each run, Pallas kernels for 57% -> 75%
where the time goes in v6:
time: 83.6 us; the launch traced here: 82.7 us
  Pallas kernels  61.6 us (74%)
  starting transfers between devices  16.1 us (19%)
  other arithmetic  3.35 us (4%)
  local copies, waits for them, and re-layouts  0.89 us (1%)
    pallas_call x1, Pallas kernels, body(): pl.pallas_call(functools.partial(adjoint_kernel, pitch, chunk_slots), out...  22.8 us
    pallas_call x1, Pallas kernels, body(): pl.pallas_call(functools.partial(forward_kernel, pitch, chunk_slots), out...  16.4 us
    all_to_all x2, starting transfers between devices, to_owners(): lax.all_to_all(blocks, ('lat', 'lon'), split_axis=0, concat_axis=0, tiled...  16.1 us
    pallas_call x1, Pallas kernels, body(): pl.pallas_call(front_kernel, out_shape=[struct(cols), struct(cols), struc...  11.1 us
    pallas_call x1, Pallas kernels, body(): pl.pallas_call(back_kernel, out_shape=[struct(cols), struct(cols), struct...  8.13 us
    pallas_call x1, Pallas kernels, body(): pl.pallas_call(finish_kernel, out_shape=jax.ShapeDtypeStruct(control.shap...  3.28 us
    convert_element_type x1, other arithmetic, body(): rounded = weighted.astype(BF16)  2.62 us
  transfers between devices with their start and end apart: 2, of which 0 were waited for; matrix products, arithmetic and copies ran while one was open for 1% of the time, Pallas kernels for 75%

profile of v6, /device:TPU:0, one launch (start us, length us, event | category | flops | bytes accessed | tf_op | source)
XLA Modules:
  0.0 82.7 jit_solution(10492162445149499084)
XLA Ops:
  0.6 7.3 %all-to-all-start = ((bf16[32,64,128]{2,1,0:T(8,128)(2,1)}), bf16[32,64,128]{2,1,0:T(8,128)(2,1)S(1)}, u32[]{:S(2)}, u32[]{:S(2)}) async-start(bf16[32,64,128]{2,1,0:T(8,128)(2,1)} %bitcast.10), calls=%async_computation | async-start | bytes 1048576 | tf_op jit(solution)/shard_map/all_to_all | solution.py:345
  7.9 0.7 iota_compare_fusion
  8.7 0.1 lt.26
  8.8 0.0 copy-start
  8.8 11.1 %front.1 = (f32[128,128]{1,0:T(8,128)}, f32[128,128]{1,0:T(8,128)}, f32[144,128]{1,0:T(8,128)}, f32[144,128]{1,0:T(8,128)}, bf16[1152,256]{1,0:T(8,128)(2,1)}, /...) custom-call(f32[128,128,128]{2,1,0:T(8,128)} %control_ref.5, f32[9,128,128]{2,1,0:T(8,128)} %corr_ref.1, ...), custom_call_target="tpu_custom_call" | custom-call | tf_op jit(solution)/shard_map/front/pallas_call | solution.py:352
  19.8 16.4 %forward.1 = f32[2048,128]{1,0:T(8,128)} custom-call(s32[1,2048]{1,0:T(1,128)} %col_ref.3, f32[1,2,2048]{2,1,0:T(2,128)} %frac_ref.3, bf16[1152,256]{1,0:T(8,128)(2,1)} %get-tuple-element.24.g_both, f32[128,128]{1,0:T(8,128)} %get-tuple-element.25.north_ref, f32[128,128]{1,0:T(8,128)} %get-tuple-element.26.south_ref, f32[144,128]{1,0:T(8,128)} %get-tuple-element.27.west_ref, ...), custom_call_target="tpu_custom_call" | custom-call | flops 2415919104 | bytes 41943040 | tf_op jit(solution)/shard_map/forward/pallas_call | solution.py:374
  36.2 0.0 all-to-all-done
  36.2 0.0 copy-done
  36.2 2.6 %fusion.2 = (bf16[2048,128]{1,0:T(8,128)(2,1)}, f32[2048,128]{1,0:T(8,128)}) fusion(f32[2048,128]{1,0:T(8,128)} %forward.1, bf16[32,64,128]{2,1,0:T(8,128)(2,1)S(1)} %all-to-all-done, f32[2048]{0:T(1024)S(1)} %bitcast.11, pred[2048]{0:T(1024)(128)(4,1)S(1)} %lt.26), kind=kLoop, calls=%fused_computation.4 | loop fusion | flops 1310720 | bytes 3155968 | tf_op jit(solution)/shard_map/convert_element_type | solution.py:396
  38.8 8.8 %all-to-all-start.1 = ((bf16[32,64,128]{2,1,0:T(8,128)(2,1)}), bf16[32,64,128]{2,1,0:T(8,128)(2,1)S(1)}, u32[]{:S(2)}, u32[]{:S(2)}) async-start(bf16[32,64,128]{2,1,0:T(8,128)(2,1)} %bitcast.4), calls=%async_computation.1 | async-start | bytes 1048576 | tf_op jit(solution)/shard_map/all_to_all | solution.py:345
  47.7 22.8 %adjoint.1 = (f32[128,128,128]{2,1,0:T(8,128)}, f32[144,128]{1,0:T(8,128)}, f32[144,128]{1,0:T(8,128)}, f32[128,128]{1,0:T(8,128)}, f32[128,128]{1,0:T(8,128)}) custom-call(s32[1,2048]{1,0:T(1,128)} %col_ref.3, f32[1,2,2048]{2,1,0:T(2,128)} %frac_ref.3, bf16[256,1152]{1,0:T(8,128)(2,1)} %get-tuple-element.22.gt_hi, ...), custom_call_target="tpu_custom_call" | custom-call | flops 2415919104 | bytes 62914560 | tf_op jit(solution)/shard_map/adjoint/pallas_call | solution.py:400
  70.5 8.1 %back.1 = (f32[128,128]{1,0:T(8,128)}, f32[128,128]{1,0:T(8,128)}, f32[128,128]{1,0:T(8,128)}, f32[128,128]{1,0:T(8,128)}, f32[8,128]{1,0:T(8,128)}, /*index=5*/...) custom-call(f32[144,128]{1,0:T(8,128)} %get-tuple-element.29.out_n, f32[144,128]{1,0:T(8,128)} %get-tuple-element.30.out_s, ...), custom_call_target="tpu_custom_call" | custom-call | tf_op jit(solution)/shard_map/back/pallas_call | solution.py:425
  78.6 3.3 %finish.1 = f32[128,128,128]{2,1,0:T(8,128)} custom-call(f32[128,128]{1,0:T(8,128)} %get-tuple-element.33.north_ref, f32[128,128]{1,0:T(8,128)} %get-tuple-element.34.south_ref, f32[128,128]{1,0:T(8,128)} %get-tuple-element.35.west_ref, f32[128,128]{1,0:T(8,128)} %get-tuple-element.36.east_ref, ...), custom_call_target="tpu_custom_call", output_to_operand_aliasing={{}: (8, {})} | custom-call | tf_op jit(solution)/shard_map/finish/pallas_call | solution.py:437
  81.9 0.0 all-to-all-done.1
  81.9 0.8 copy.13
Async XLA Ops:
  0.6 35.6 %all-to-all-start = ((bf16[32,64,128]{2,1,0:T(8,128)(2,1)}), bf16[32,64,128]{2,1,0:T(8,128)(2,1)S(1)}, u32[]{:S(2)}, u32[]{:S(2)}) async-start(bf16[32,64,128]{2,1,0:T(8,128)(2,1)} %bitcast.10), calls=%async_computation | async-start | bytes 1048576 | tf_op jit(solution)/shard_map/all_to_all | solution.py:345
  8.8 27.5 %copy-start = (f32[1,2048]{1,0:T(1,128)S(1)}, f32[1,2048]{1,0:T(1,128)}, u32[]{:S(2)}) copy-start(f32[1,2048]{1,0:T(1,128)} %param.15) | copy-start | bytes 24580
  38.8 43.1 %all-to-all-start.1 = ((bf16[32,64,128]{2,1,0:T(8,128)(2,1)}), bf16[32,64,128]{2,1,0:T(8,128)(2,1)S(1)}, u32[]{:S(2)}, u32[]{:S(2)}) async-start(bf16[32,64,128]{2,1,0:T(8,128)(2,1)} %bitcast.4), calls=%async_computation.1 | async-start | bytes 1048576 | tf_op jit(solution)/shard_map/all_to_all | solution.py:345

commit v7 on v4

--- a/solution.py
+++ b/solution.py
@@ -125,7 +125,6 @@
         return c
 
     lax.fori_loop(1, rows + 1, clear, 0)
-    fetch.wait()
     flat = pad.reshape((rows + 2) * pitch, 128)
 
     def chunk(n, carry):
@@ -171,6 +170,11 @@
             return c
 
         mix(0, patches_a)
+
+        @pl.when(n == 0)
+        def _():
+            fetch.wait()
+
         lax.fori_loop(0, chunk_slots // 16, pair, 0, unroll=2)
         return carry
 

time: 82.9 us -> 82.1 us (level)
  Pallas kernels: 63.4 us -> 62.5 us
    pallas_call x1, Pallas kernels: 23.7 us -> 22.8 us  [body(): pl.pallas_call(functools.partial(adjoint_kernel, pitch, chunk_slots), out...]
  transfers between devices with their start and end apart: 2 -> 2, of which waited for: 1 -> 1; matrix products, arithmetic and copies ran while one was open for 0% -> 0% of each run, Pallas kernels for 57% -> 56%
where the time goes in v7:
time: 82.1 us; the launch traced here: 81.2 us
  Pallas kernels  62.5 us (76%)
  starting transfers between devices  11.7 us (14%)
  waiting for transfers between devices  4.76 us (6%)
  local copies, waits for them, and re-layouts  1.59 us (2%)
    pallas_call x1, Pallas kernels, body(): pl.pallas_call(functools.partial(adjoint_kernel, pitch, chunk_slots), out...  22.8 us
    pallas_call x1, Pallas kernels, body(): pl.pallas_call(functools.partial(forward_kernel, pitch, chunk_slots), out...  16.7 us
    all_to_all x2, starting transfers between devices, to_owners(): lax.all_to_all(blocks, ('lat', 'lon'), split_axis=0, concat_axis=0, tiled...  11.7 us
    pallas_call x1, Pallas kernels, body(): pl.pallas_call(front_kernel, out_shape=[struct(cols), struct(cols), struc...  11.6 us
    pallas_call x1, Pallas kernels, body(): pl.pallas_call(back_kernel, out_shape=[struct(cols), struct(cols), struct...  8.14 us
    all_to_all x2, waiting for transfers between devices, to_owners(): lax.all_to_all(blocks, ('lat', 'lon'), split_axis=0, concat_axis=0, tiled...  4.76 us
    pallas_call x1, Pallas kernels, body(): pl.pallas_call(finish_kernel, out_shape=jax.ShapeDtypeStruct(control.shap...  3.28 us
  transfers between devices with their start and end apart: 2, of which 1 were waited for; matrix products, arithmetic and copies ran while one was open for 0% of the time, Pallas kernels for 56%

profile of v7, /device:TPU:0, one launch (start us, length us, event | category | flops | bytes accessed | tf_op | source)
XLA Modules:
  0.0 81.2 jit_solution(17638449616871641698)
XLA Ops:
  0.6 7.3 %all-to-all-start = ((bf16[32,64,128]{2,1,0:T(8,128)(2,1)}), bf16[32,64,128]{2,1,0:T(8,128)(2,1)S(1)}, u32[]{:S(2)}, u32[]{:S(2)}) async-start(bf16[32,64,128]{2,1,0:T(8,128)(2,1)} %bitcast.6), calls=%async_computation | async-start | bytes 1048576 | tf_op jit(solution)/shard_map/all_to_all | solution.py:355
  7.9 11.6 %front.1 = (f32[128,128]{1,0:T(8,128)}, f32[128,128]{1,0:T(8,128)}, f32[144,128]{1,0:T(8,128)}, f32[144,128]{1,0:T(8,128)}, bf16[1152,256]{1,0:T(8,128)(2,1)}, /...) custom-call(f32[128,128,128]{2,1,0:T(8,128)} %control_ref.5, f32[9,128,128]{2,1,0:T(8,128)} %corr_ref.1, ...), custom_call_target="tpu_custom_call" | custom-call | tf_op jit(solution)/shard_map/front/pallas_call | solution.py:362
  19.5 4.8 %all-to-all-done = bf16[32,64,128]{2,1,0:T(8,128)(2,1)S(1)} async-done(((bf16[32,64,128]{2,1,0:T(8,128)(2,1)}), bf16[32,64,128]{2,1,0:T(8,128)(2,1)S(1)}, u32[]{:S(2)}, u32[]{:S(2)}) %all-to-all-start) | async-done | bytes 524320 | tf_op jit(solution)/shard_map/all_to_all | solution.py:355
  24.3 0.0 copy-start
  24.3 0.8 copy-done
  25.1 16.7 %forward.1 = (f32[2048,128]{1,0:T(8,128)}, bf16[2048,128]{1,0:T(8,128)(2,1)}) custom-call(s32[1,2048]{1,0:T(1,128)} %col_ref.3, s32[1,32]{1,0:T(1,128)} %count_ref.1, f32[1,2,2048]{2,1,0:T(2,128)} %frac_ref.3, f32[1,2048]{1,0:T(1,128)} %rinv_ref.1, bf16[2048,128]{1,0:T(8,128)(2,1)} %bitcast.4, bf16[1152,256]{1,0:T(8,128)(2,1)} %get-tuple-element.26.g_both, ...), custom_call_target="tpu_custom_call" | custom-call | flops 2415919104 | bytes 41943040 | tf_op jit(solution)/shard_map/forward/pallas_call | solution.py:384
  41.8 4.4 %all-to-all-start.1 = ((bf16[32,64,128]{2,1,0:T(8,128)(2,1)}), bf16[32,64,128]{2,1,0:T(8,128)(2,1)S(1)}, u32[]{:S(2)}, u32[]{:S(2)}) async-start(bf16[32,64,128]{2,1,0:T(8,128)(2,1)} %bitcast.7), calls=%async_computation.1 | async-start | bytes 1048576 | tf_op jit(solution)/shard_map/all_to_all | solution.py:355
  46.2 22.8 %adjoint.1 = (f32[128,128,128]{2,1,0:T(8,128)}, f32[144,128]{1,0:T(8,128)}, f32[144,128]{1,0:T(8,128)}, f32[128,128]{1,0:T(8,128)}, f32[128,128]{1,0:T(8,128)}) custom-call(s32[1,2048]{1,0:T(1,128)} %col_ref.3, f32[1,2,2048]{2,1,0:T(2,128)} %frac_ref.3, bf16[256,1152]{1,0:T(8,128)(2,1)} %get-tuple-element.24.gt_hi, ...), custom_call_target="tpu_custom_call" | custom-call | flops 2415919104 | bytes 62914560 | tf_op jit(solution)/shard_map/adjoint/pallas_call | solution.py:405
  69.0 8.1 %back.1 = (f32[128,128]{1,0:T(8,128)}, f32[128,128]{1,0:T(8,128)}, f32[128,128]{1,0:T(8,128)}, f32[128,128]{1,0:T(8,128)}, f32[8,128]{1,0:T(8,128)}, /*index=5*/...) custom-call(f32[144,128]{1,0:T(8,128)} %get-tuple-element.32.out_n, f32[144,128]{1,0:T(8,128)} %get-tuple-element.33.out_s, ...), custom_call_target="tpu_custom_call" | custom-call | tf_op jit(solution)/shard_map/back/pallas_call | solution.py:430
  77.1 3.3 %finish.1 = f32[128,128,128]{2,1,0:T(8,128)} custom-call(f32[128,128]{1,0:T(8,128)} %get-tuple-element.36.north_ref, f32[128,128]{1,0:T(8,128)} %get-tuple-element.37.south_ref, f32[128,128]{1,0:T(8,128)} %get-tuple-element.38.west_ref, f32[128,128]{1,0:T(8,128)} %get-tuple-element.39.east_ref, ...), custom_call_target="tpu_custom_call", output_to_operand_aliasing={{}: (8, {})} | custom-call | tf_op jit(solution)/shard_map/finish/pallas_call | solution.py:442
  80.4 0.0 all-to-all-done.1
  80.4 0.8 copy.13
Async XLA Ops:
  0.6 23.7 %all-to-all-start = ((bf16[32,64,128]{2,1,0:T(8,128)(2,1)}), bf16[32,64,128]{2,1,0:T(8,128)(2,1)S(1)}, u32[]{:S(2)}, u32[]{:S(2)}) async-start(bf16[32,64,128]{2,1,0:T(8,128)(2,1)} %bitcast.6), calls=%async_computation | async-start | bytes 1048576 | tf_op jit(solution)/shard_map/all_to_all | solution.py:355
  24.3 0.8 copy-start
  41.8 38.6 %all-to-all-start.1 = ((bf16[32,64,128]{2,1,0:T(8,128)(2,1)}), bf16[32,64,128]{2,1,0:T(8,128)(2,1)S(1)}, u32[]{:S(2)}, u32[]{:S(2)}) async-start(bf16[32,64,128]{2,1,0:T(8,128)(2,1)} %bitcast.7), calls=%async_computation.1 | async-start | bytes 1048576 | tf_op jit(solution)/shard_map/all_to_all | solution.py:355
